TPU v7x, 32 devices: a whole 2x2x4 slice. The times are simulated.
32 devices in a mesh: groups: 2 (over x), tensor: 16 (over z, y, core).
Axes of the slice: x: 2, y: 2, z: 4, core: 2. Of those that a mesh axis runs over, the one named last changes fastest.
Arguments:
- hidden: bfloat16 [384, 16384], P('groups', 'tensor'), parts along dimension 0, may hold values from -6 to 6
- w_query: bfloat16 [16384, 8192], P(None, 'tensor'), may hold values from -0.046875 to 0.046875
- w_out: bfloat16 [8192, 16384], P('tensor'), may hold values from -0.09375 to 0.09375
- new_kv: bfloat16 [384, 2, 4, 128], P(('groups', 'tensor')), parts along dimension 0, may hold values from -6 to 6
- prefix_kv: bfloat16 [32, 3, 2, 4, 512, 128], P(('groups', 'tensor')), parts along dimension 0, may hold values from -700 to 700
- suffix_kv: bfloat16 [384, 2, 4, 256, 128], P(('groups', 'tensor')), parts along dimension 0, may hold values from -6 to 6
- parents: int32 [384], P(('groups', 'tensor')), parts along dimension 0, may hold values from 0 to 7
- lengths: int32 [384], P(('groups', 'tensor')), parts along dimension 0, may hold values from 1 to 256, 36864 in all
Outputs:
- attended: bfloat16 [384, 16384], P('groups', 'tensor'), parts along dimension 0
There are 2 independent parts, one for each index of `groups`. A program takes and returns all parts, laid end to end along the dimension named above; an argument that names none is the same for every part. Nothing has to cross between parts.
Inputs may be any that keep to these rules, and one draw needn't show every extreme that they name: `lengths`: some page is full.
All inputs are finite; a program needn't handle non-finite values. No bound on the sum of `lengths` on one device may be relied on, other than what follows from the above.
Results may differ from a plain program's by a relative error of at most 0.02.
The roundings to bfloat16 on the way count: a program that leaves them out, or rounds other values in their place, can miss the bound.
Values may be sent and summed in bfloat16 or wider, within the bound.
No kernel may reach another device: no remote copies, remote signals or barrier semaphores. Data moves between devices by JAX's collectives and lax.ppermute only.
A program may use at most 192 MiB of HBM per device.

v0:
```python
import jax
import jax.numpy as jnp
from jax import lax
from jax.sharding import PartitionSpec as P

HEADS = 64
KV = 4
HD = 128
BEAMS = 8


big_negative = -1e30
rope_base = 500000.0


def swapped(block, axis, apart):
    count = lax.axis_size(axis)
    route = []
    for low in range(count):
        high = low | 1 << apart
        if high != low and high < count:
            route += [(low, high), (high, low)]
    return lax.ppermute(block, axis, route)


def rotate(queries, position):
    half_size = HD // 2
    frequency = rope_base ** (-jnp.arange(half_size, dtype=jnp.float32) * 2.0 / HD)
    angles = position.astype(jnp.float32)[..., None, None] * frequency
    cosine = jnp.cos(angles)
    sines = jnp.sin(angles)
    entries = queries.astype(jnp.float32)
    lower_half = entries[..., :half_size]
    upper_half = entries[..., half_size:]
    turned = jnp.concatenate(
        [lower_half * cosine - upper_half * sines, upper_half * cosine + lower_half * sines],
        axis=-1,
    )
    return (turned * HD ** (-0.5)).astype(jnp.bfloat16)


def shared_part(grouped, key_block, value_block):
    scores = jnp.einsum("pbkge,pkne->pbkgn", grouped, key_block, preferred_element_type=jnp.float32)
    highest = jnp.max(scores, axis=-1)
    weights = jnp.exp(scores - highest[..., None])
    weight_sum = jnp.sum(weights, axis=-1)
    weighted = jnp.einsum(
        "pbkgn,pkne->pbkge",
        weights.astype(jnp.bfloat16),
        value_block,
        preferred_element_type=jnp.float32,
    )
    return (highest, weight_sum, weighted)


def own_part(grouped, key_block, value_block, usable):
    scores = jnp.einsum(
        "pbkge,pbkse->pbkgs", grouped, key_block, preferred_element_type=jnp.float32
    )
    usable_mask = usable[:, :, None, None, :]
    highest = jnp.max(jnp.where(usable_mask, scores, big_negative), axis=-1)
    weights = jnp.where(usable_mask, jnp.exp(scores - highest[..., None]), 0.0)
    weight_sum = jnp.sum(weights, axis=-1)
    weighted = jnp.einsum(
        "pbkgs,pbkse->pbkge",
        weights.astype(jnp.bfloat16),
        value_block,
        preferred_element_type=jnp.float32,
    )
    return (highest, weight_sum, weighted)


def combine(left_state, right_state):
    highest = jnp.maximum(left_state[0], right_state[0])
    left_factor = jnp.exp(left_state[0] - highest)
    right_factor = jnp.exp(right_state[0] - highest)
    weight_sum = left_state[1] * left_factor + right_state[1] * right_factor
    weighted = left_state[2] * left_factor[..., None] + right_state[2] * right_factor[..., None]
    return (highest, weight_sum, weighted)


def body(hidden, w_query, w_out, new_kv, prefix_kv, suffix_kv, parents, lengths):
    pair_side = lax.axis_index("tensor") % 2
    rows_here = new_kv.shape[0]
    half_beams = BEAMS // 2
    prompts_here = rows_here // half_beams
    prefix_len = 2 * prefix_kv.shape[4]
    page_size = suffix_kv.shape[3]
    per_kv = HEADS // KV

    def in_order(own_part_rows, far_rows, along):
        lower_part = jnp.where(pair_side == 0, own_part_rows, far_rows)
        upper_part = jnp.where(pair_side == 0, far_rows, own_part_rows)
        return jnp.concatenate([lower_part, upper_part], axis=along)

    query = jnp.dot(
        lax.all_gather(hidden, "tensor", axis=1, tiled=True),
        w_query,
        preferred_element_type=jnp.float32,
    ).astype(jnp.bfloat16)
    local_q = lax.all_to_all(query, "tensor", split_axis=0, concat_axis=1, tiled=True)
    local_q = local_q.reshape(prompts_here, half_beams, HEADS, HD)
    own_par = parents.reshape(prompts_here, half_beams)
    own_len = lengths.reshape(prompts_here, half_beams)
    own_pages = suffix_kv.reshape(prompts_here, half_beams, 2, KV, page_size, HD)
    new_pair = new_kv.reshape(prompts_here, half_beams, 2, KV, HD)
    positions = jnp.arange(page_size)
    far_prefix, far_pages, far_len = swapped((prefix_kv, suffix_kv, lengths), "tensor", 0)
    prefix_full = in_order(prefix_kv[0], far_prefix[0], 3)
    pages_all = in_order(own_pages, far_pages.reshape(own_pages.shape), 1)
    len_all = in_order(own_len, far_len.reshape(own_len.shape), 1)
    chosen = jnp.take_along_axis(pages_all, own_par[:, :, None, None, None, None], axis=1)
    page_len = jnp.take_along_axis(len_all, own_par, axis=1)
    grouped = rotate(local_q, prefix_len + page_len).reshape(
        prompts_here, half_beams, KV, per_kv, HD
    )
    prefix_state = shared_part(grouped, prefix_full[:, 0], prefix_full[:, 1])
    usable = positions[None, None, :] < page_len[:, :, None]
    suffix_state = own_part(grouped, chosen[:, :, 0], chosen[:, :, 1], usable)
    merged = combine(prefix_state, suffix_state)
    new_scores = jnp.einsum(
        "pbkge,pbke->pbkg", grouped, new_pair[:, :, 0], preferred_element_type=jnp.float32
    )
    new_values = jnp.broadcast_to(
        new_pair[:, :, 1].astype(jnp.float32)[:, :, :, None, :], grouped.shape
    )
    new_state = (new_scores, jnp.ones_like(new_scores), new_values)
    highest, weight_sum, weighted = combine(merged, new_state)
    heads_out = (
        (weighted / weight_sum[..., None]).astype(jnp.bfloat16).reshape(rows_here, HEADS * HD)
    )
    heads_view = lax.all_to_all(heads_out, "tensor", split_axis=1, concat_axis=0, tiled=True)
    projected = jnp.dot(heads_view, w_out, preferred_element_type=jnp.float32)
    summed = lax.psum_scatter(
        projected.astype(jnp.bfloat16), "tensor", scatter_dimension=1, tiled=True
    )
    return summed


def solution(mesh):
    return jax.shard_map(
        body,
        mesh=mesh,
        in_specs=(
            P("groups", "tensor"),
            P(None, "tensor"),
            P("tensor", None),
            P(("groups", "tensor"), None, None, None),
            P(("groups", "tensor"), None, None, None, None, None),
            P(("groups", "tensor"), None, None, None, None),
            P(("groups", "tensor")),
            P(("groups", "tensor")),
        ),
        out_specs=P("groups", "tensor"),
        check_vma=False,
    )
```

profile of v0, /device:TPU:0, one launch (start us, length us, event | category | flops | bytes accessed | tf_op | source)
XLA Modules:
  0.0 227.0 jit_solution(14612947954421246856)
XLA Ops:
  7.8 3.9 %copy.48 = bf16[1,3,2,4,512,128]{5,4,3,1,2,0:T(8,128)(2,1)} copy(bf16[1,3,2,4,512,128]{5,4,3,2,1,0:T(8,128)(2,1)} %param.12) | data formatting | bytes 6291456 | tf_op args[4]
  13.7 3.9 %collective-permute-done.1 = s32[12]{0:T(128)S(1)} collective-permute-done((s32[12]{0:T(128)S(1)}, s32[12]{0:T(128)S(1)}, u32[]{:S(2)}, u32[]{:S(2)}) %collective-permute-start.1) | collective-permute-done | bytes 80 | tf_op jit(solution)/shard_map/ppermute | solution.py:23
  19.5 3.0 %collective-permute-done = bf16[1,3,2,4,512,128]{5,4,3,1,2,0:T(8,128)(2,1)} collective-permute-done((bf16[1,3,2,4,512,128]{5,4,3,1,2,0:T(8,128)(2,1)}, bf16[1,3,2,4,512,128]{5,4,3,1,2,0:T(8,128)(2,1)}, u32[]{:S(2)}, u32[]{:S(2)}) %collective-permute-start) | collective-permute-done | bytes 3145760 | tf_op jit(solution)/shard_map/ppermute | solution.py:23
  22.4 5.0 %select_bitcast_fusion.1 = (bf16[3,2,4,512,128]{4,3,2,0,1:T(8,128)(2,1)}, bf16[3,2,4,512,128]{4,3,2,0,1:T(8,128)(2,1)}) fusion(bf16[1,3,2,4,512,128]{5,4,3,1,2,0:T(8,128)(2,1)} %collective-permute-done, pred[]{:T(512)S(6)} %eq.4, bf16[1,3,2,4,512,128]{5,4,3,2,1,0:T(8,128)(2,1)S(1)} %copy-done), kind=kLoop, calls=%fused_computation.24 | loop fusion | flops 3145728 | bytes 12582913 | tf_op jit(solution)/shard_map/jit(_where)/select_n | solution.py:92
  27.5 3.9 %broadcast_select_fusion.1 = (bf16[12,2,4,256,128]{4,3,2,1,0:T(8,128)(2,1)S(1)}, bf16[12,2,4,256,128]{4,3,2,1,0:T(8,128)(2,1)S(1)}) fusion(bf16[12,2,4,256,128]{4,3,2,1,0:T(8,128)(2,1)S(1)} %bitcast.116, bf16[12,2,4,256,128]{4,3,2,1,0:T(8,128)(2,1)} %collective-permute-done.2, pred[]{:T(512)S(6)} %eq.4), kind=kLoop, calls=%fused_computation.7 | loop fusion | flops 6291456 | bytes 25165824 | tf_op jit(solution)/shard_map/jit(_where)/select_n | solution.py:92
  31.4 5.3 %pad_maximum_fusion = bf16[3,8,2,4,256,128]{5,4,3,2,1,0:T(8,128)(2,1)} fusion(bf16[3,4,2,4,256,128]{5,4,3,2,1,0:T(8,128)(2,1)S(1)} %bitcast.112, bf16[3,4,2,4,256,128]{5,4,3,2,1,0:T(8,128)(2,1)S(1)} %bitcast.111), kind=kLoop, calls=%fused_computation.3 | loop fusion | flops 6291456 | bytes 25165824 | tf_op jit(solution)/shard_map/concatenate | solution.py:94
  36.6 8.8 %gather_fusion.1 = bf16[12,2,4,256,128]{4,3,2,1,0:T(8,128)(2,1)} fusion(bf16[3,8,2,4,256,128]{5,4,3,2,1,0:T(8,128)(2,1)} %pad_maximum_fusion, s32[12]{0:T(128)S(1)} %reshape.196), kind=kCustom, calls=%fused_computation.1 | custom fusion | bytes 12583008 | tf_op jit(solution)/shard_map/jit(take_along_axis)/gather | solution.py:112
  45.4 6.2 %copy.53 = bf16[12,2,4,256,128]{4,3,2,0,1:T(8,128)(2,1)} copy(bf16[12,2,4,256,128]{4,3,2,1,0:T(8,128)(2,1)} %gather_fusion.1) | data formatting | bytes 12582912 | tf_op jit(solution)/shard_map/jit(take_along_axis)/gather | solution.py:112
  51.7 22.6 %all-gather.2.cloned.1.call-done = bf16[192,16384]{1,0:T(8,128)(2,1)} async-done(((bf16[192,1024]{1,0:T(8,128)(2,1)}), bf16[192,16384]{1,0:T(8,128)(2,1)}) %all-gather.2.cloned.1.call-update) | async-done | bytes 6291472 | tf_op jit(solution)/shard_map/all_gather | solution.py:97
  74.2 11.0 %convolution_convert_fusion.1 = bf16[192,512]{1,0:T(8,128)(2,1)S(1)} fusion(bf16[192,16384]{1,0:T(8,128)(2,1)} %all-gather.2.cloned.1.call-done, bf16[16384,512]{1,0:T(8,128)(2,1)} %param.9), kind=kOutput, calls=%fused_computation.35 | convolution fusion | flops 3221323776 | bytes 23265280 | tf_op jit(solution)/shard_map/dot_general | solution.py:96
  85.2 0.7 all_to_all.24
  86.0 3.5 %all-to-all-start = ((bf16[16,12,512]{2,1,0:T(8,128)(2,1)}), bf16[16,12,512]{2,1,0:T(8,128)(2,1)S(1)}, u32[]{:S(2)}, u32[]{:S(2)}) async-start(bf16[16,12,512]{2,1,0:T(8,128)(2,1)} %all_to_all.24), calls=%async_computation | async-start | bytes 524288 | tf_op jit(solution)/shard_map/all_to_all | solution.py:101
  89.6 6.1 %broadcast_select_fusion.2 = bf16[3,4,2,4,256,128]{5,4,3,1,0,2:T(8,128)(2,1)} fusion(bf16[3,4,2,4,256,128]{5,4,3,1,0,2:T(8,128)(2,1)} %bitcast.110, pred[3,4]{1,0:T(4,128)(4,1)S(1)} %get-tuple-element.12), kind=kLoop, calls=%fused_computation.8 | loop fusion | flops 3145728 | bytes 12582924 | tf_op jit(solution)/shard_map/jit(take_along_axis)/select_n | solution.py:112
  95.7 3.8 %all-to-all-done = bf16[16,12,512]{2,1,0:T(8,128)(2,1)S(1)} async-done(((bf16[16,12,512]{2,1,0:T(8,128)(2,1)}), bf16[16,12,512]{2,1,0:T(8,128)(2,1)S(1)}, u32[]{:S(2)}, u32[]{:S(2)}) %all-to-all-start) | async-done | bytes 196640 | tf_op jit(solution)/shard_map/all_to_all | solution.py:101
  99.6 1.0 copy.50
  100.6 1.0 reshape.194
  101.6 1.0 multiply_subtract_fusion
  102.8 0.9 fusion.58
  103.7 2.9 %select_reduce_fusion = (f32[3,4,4,16]{3,2,1,0:T(4,128)S(1)}, f32[3,4,4,16,256]{4,3,2,1,0:T(8,128)S(1)}) fusion(pred[3,4,256]{2,1,0:T(4,128)(4,1)S(1)} %iota_compare_fusion, bf16[3,4,2,4,256,128]{5,4,3,1,0,2:T(8,128)(2,1)} %broadcast_select_fusion.2, bf16[3,4,4,16,128]{4,3,1,2,0:T(8,128)(2,1)S(1)} %fusion.56), kind=kOutput, calls=%fused_computation.39 | convolution fusion | flops 50724096 | bytes 4134912 | tf_op jit(solution)/shard_map/pbkge,pbkse->pbkgs/dot_general | solution.py:57
  107.0 1.3 bitcast_reduce_fusion
  110.2 1.3 fusion.49
  111.7 12.8 %all_to_all.32 = bf16[12,16,512]{2,0,1:T(8,128)(2,1)S(1)} all-to-all(bf16[12,16,512]{2,0,1:T(8,128)(2,1)S(1)} %copy.61), channel_id=1, replica_groups=mesh['groups'=2,'tensor'=16] {'tensor'}, dimensions={1} | all-to-all | bytes 393216 | tf_op jit(solution)/shard_map/all_to_all | solution.py:132
  124.6 11.9 %convolution_convert_fusion = bf16[192,16384]{1,0:T(8,128)(2,1)} fusion(bf16[192,512]{1,0:T(8,128)(2,1)S(1)} %all_to_all.29, bf16[512,16384]{1,0:T(8,128)(2,1)} %param.10), kind=kOutput, calls=%fused_computation.2 | convolution fusion | flops 3224371200 | bytes 23265280 | tf_op jit(solution)/shard_map/dot_general | solution.py:133
  136.5 83.7 %reduce-scatter.2.cloned.1.call-done = bf16[192,1024]{1,0:T(8,128)(2,1)} async-done(((bf16[192,16384]{1,0:T(8,128)(2,1)}), bf16[192,1024]{1,0:T(8,128)(2,1)}) %reduce-scatter.2.cloned.1.call-update) | async-done | bytes 393232 | tf_op jit(solution)/shard_map/reduce_scatter | solution.py:134
  (58 shorter events, 7.9 us)
Async XLA Ops:
  6.5 15.9 %copy-start = (bf16[1,3,2,4,512,128]{5,4,3,2,1,0:T(8,128)(2,1)S(1)}, bf16[1,3,2,4,512,128]{5,4,3,2,1,0:T(8,128)(2,1)}, u32[]{:S(2)}) copy-start(bf16[1,3,2,4,512,128]{5,4,3,2,1,0:T(8,128)(2,1)} %param.12) | copy-start | bytes 9437188
  6.5 5.3 %copy-start.6 = (s32[12]{0:T(128)S(1)}, s32[12]{0:T(128)}, u32[]{:S(2)}) copy-start(s32[12]{0:T(128)} %param.15) | copy-start | bytes 148
  6.5 5.6 %copy-start.5 = (s32[12]{0:T(128)S(1)}, s32[12]{0:T(128)}, u32[]{:S(2)}) copy-start(s32[12]{0:T(128)} %param.14) | copy-start | bytes 148
  6.5 5.9 %copy-start.3 = (bf16[12,2,4,128]{3,2,1,0:T(4,128)(2,1)S(1)}, bf16[12,2,4,128]{3,2,1,0:T(4,128)(2,1)}, u32[]{:S(2)}) copy-start(bf16[12,2,4,128]{3,2,1,0:T(4,128)(2,1)} %param.11) | copy-start | bytes 73732
  6.5 67.7 %all-gather.2.cloned.1.call-start = ((), (), s32[]{:S(2)}) async-start(), calls=%async_computation.3 | async-start | bytes 6684672 | tf_op jit(solution)/shard_map/all_gather | solution.py:97
  7.3 20.2 %collective-permute-start.2 = (bf16[12,2,4,256,128]{4,3,2,1,0:T(8,128)(2,1)}, bf16[12,2,4,256,128]{4,3,2,1,0:T(8,128)(2,1)}, u32[]{:S(2)}, u32[]{:S(2)}) collective-permute-start(bf16[12,2,4,256,128]{4,3,2,1,0:T(8,128)(2,1)} %param.13), channel_id=1, source_target_pairs={{0,1},{1,0},{2,3},{3,2},{4,5},{5,4},{6,7},{7,6},{8,9},{9,8},{10,11... | collective-permute-start | bytes 18874376 | tf_op jit(solution)/shard_map/ppermute | solution.py:23
  11.6 10.8 %collective-permute-start = (bf16[1,3,2,4,512,128]{5,4,3,1,2,0:T(8,128)(2,1)}, bf16[1,3,2,4,512,128]{5,4,3,1,2,0:T(8,128)(2,1)}, u32[]{:S(2)}, u32[]{:S(2)}) collective-permute-start(bf16[1,3,2,4,512,128]{5,4,3,1,2,0:T(8,128)(2,1)} %copy.48), channel_id=1, source_target_pairs={{0,1},{1,0},{2,3},{3,2},{4,5},{5,4},{6,7},{7,6},{8,9},{9,8},{10,11... | collective-permute-start | bytes 9437192 | tf_op jit(solution)/shard_map/ppermute | solution.py:23
  11.8 5.7 %collective-permute-start.1 = (s32[12]{0:T(128)S(1)}, s32[12]{0:T(128)S(1)}, u32[]{:S(2)}, u32[]{:S(2)}) collective-permute-start(s32[12]{0:T(128)S(1)} %copy-done.6), channel_id=1, source_target_pairs={{0,1},{1,0},{2,3},{3,2},{4,5},{5,4},{6,7},{7,6},{8,9},{9,8},{10,11... | collective-permute-start | bytes 152 | tf_op jit(solution)/shard_map/ppermute | solution.py:23
  18.7 8.7 %slice-start.2 = ((s8[6291456]{0:T(1024)(128)(4,1)}), s8[4194304]{0:T(1024)(128)(4,1)S(1)}, s32[]{:S(2)}) async-start(s8[6291456]{0:T(1024)(128)(4,1)} %bitcast.115), calls=%async_computation.7 | async-start | bytes 8388608
  19.5 8.0 %slice-start.3 = ((s8[6291456]{0:T(1024)(128)(4,1)}), s8[2097152]{0:T(1024)(128)(4,1)S(1)}, s32[]{:S(2)}) async-start(s8[6291456]{0:T(1024)(128)(4,1)} %bitcast.115), calls=%async_computation.8 | async-start | bytes 4194304
  86.0 13.5 %all-to-all-start = ((bf16[16,12,512]{2,1,0:T(8,128)(2,1)}), bf16[16,12,512]{2,1,0:T(8,128)(2,1)S(1)}, u32[]{:S(2)}, u32[]{:S(2)}) async-start(bf16[16,12,512]{2,1,0:T(8,128)(2,1)} %all_to_all.24), calls=%async_computation | async-start | bytes 524288 | tf_op jit(solution)/shard_map/all_to_all | solution.py:101
  89.5 130.6 %reduce-scatter.2.cloned.1.call-start = ((), (), s32[]{:S(2)}) async-start(), calls=%async_computation.4 | async-start | bytes 6684672 | tf_op jit(solution)/shard_map/reduce_scatter | solution.py:134
  95.7 11.3 %copy-start.1 = (bf16[3,2,4,512,128]{4,3,2,0,1:T(8,128)(2,1)S(1)}, bf16[3,2,4,512,128]{4,3,2,0,1:T(8,128)(2,1)}, u32[]{:S(2)}) copy-start(bf16[3,2,4,512,128]{4,3,2,0,1:T(8,128)(2,1)} %get-tuple-element.15) | copy-start | bytes 9437188
  101.6 5.4 %copy-start.2 = (bf16[3,2,4,512,128]{4,3,2,0,1:T(8,128)(2,1)S(1)}, bf16[3,2,4,512,128]{4,3,2,0,1:T(8,128)(2,1)}, u32[]{:S(2)}) copy-start(bf16[3,2,4,512,128]{4,3,2,0,1:T(8,128)(2,1)} %get-tuple-element.16) | copy-start | bytes 9437188
  106.6 2.5 %slice-start = ((s8[6291456]{0:T(1024)(128)(4,1)}), s8[4194304]{0:T(1024)(128)(4,1)S(1)}, s32[]{:S(2)}) async-start(s8[6291456]{0:T(1024)(128)(4,1)} %bitcast.113), calls=%async_computation.5 | async-start | bytes 8388608
  107.0 2.6 %slice-start.1 = ((s8[6291456]{0:T(1024)(128)(4,1)}), s8[2097152]{0:T(1024)(128)(4,1)S(1)}, s32[]{:S(2)}) async-start(s8[6291456]{0:T(1024)(128)(4,1)} %bitcast.113), calls=%async_computation.6 | async-start | bytes 4194304
  108.4 1.8 copy-start.4
Sparse Core Ops, SparseCore 0:
  9.6 64.6 all-gather.1
  136.6 83.5 reduce-scatter.1
where the time goes:
time: 228 us; the launch traced here: 227 us
  waiting for transfers between devices  118 us (52%)
  matrix products  29.8 us (13%)
  local copies, waits for them, and re-layouts  24.4 us (11%)
  other arithmetic  24.1 us (11%)
  between operations  13.6 us (6%)
  blocking collectives  12.8 us (6%)
  starting transfers between devices  4.64 us (2%)
    reduce_scatter x1, waiting for transfers between devices, body(): lax.psum_scatter(projected.astype(jnp.bfloat16), 'tensor', scatter_dimens...  83.7 us
    all_gather x1, waiting for transfers between devices, body(): lax.all_gather(hidden, 'tensor', axis=1, tiled=True)  22.6 us
    gather x2, local copies, waits for them, and re-layouts, body(): jnp.take_along_axis(pages_all, own_par[:, :, None, None, None, None], axi...  15 us
    all_to_all x1, blocking collectives, body(): lax.all_to_all(heads_out, 'tensor', split_axis=1, concat_axis=0, tiled=True)  12.8 us
    dot_general x1, matrix products, body(): projected = jnp.dot(heads_view, w_out, preferred_element_type=jnp.float32)  11.9 us
    dot_general x1, matrix products, body(): jnp.dot(lax.all_gather(hidden, 'tensor', axis=1, tiled=True), w_query, pr...  11 us
    select_n x3, other arithmetic, in_order(): lower_part = jnp.where(pair_side == 0, own_part_rows, far_rows)  8.91 us
    ppermute x3, waiting for transfers between devices, swapped(): return lax.ppermute(block, axis, route)  6.88 us
  transfers between devices with their start and end apart: 6, of which 5 were waited for; matrix products, arithmetic and copies ran while one was open for 19% of the time, Pallas kernels for 0%

commit v1 on v0

v1 whole, which is shorter than its diff:
```python
import functools

import jax
import jax.numpy as jnp
from jax import lax
from jax.experimental import pallas as pl
from jax.experimental.pallas import tpu as pltpu
from jax.sharding import PartitionSpec as P

HEADS = 64
KV = 4
HD = 128
BEAMS = 8
HALF = BEAMS // 2

rope_base = 500000.0
big_negative = -1e30
f32 = jnp.float32
bf16 = jnp.bfloat16
MIB = 1024 * 1024
VMEM_LIMIT = 48 * MIB


def ring_chips(count):
    if count == 8:
        return [0, 2, 4, 6, 7, 5, 3, 1]
    return list(range(count))


def send(block, route):
    return lax.ppermute(block, "tensor", route)


def tied(*values):
    return lax.optimization_barrier(values)


def along(order, step):
    count = len(order)
    return [
        (2 * order[i] + c, 2 * order[(i + step) % count] + c)
        for i in range(count)
        for c in range(2)
    ]


def make_plan(order, hops):
    chips = len(order)
    arrive = [0] + [d for s in range(1, hops) for d in (-s, s)] + [hops]
    leave = [hops] + [d for s in range(hops - 1, 0, -1) for d in (s, -s)] + [0]
    rows = []
    for t in range(2 * chips):
        at = order.index(t // 2)
        rows.append([order[(at + d) % chips] for d in arrive + leave] + [t % 2])
    return jnp.asarray(rows, jnp.int32)


def split_kernel(chips, by_rows, plan_ref, whole, part, buf, in_sems, out_sems):
    other = 1 - plan_ref[2 * chips]
    size = (part.shape[0] if by_rows else part.shape[1]) // chips
    ins, outs = [], []
    for i in range(chips):
        start = pl.multiple_of((2 * i + other) * size, size)
        if by_rows:
            source, target = whole.at[pl.ds(start, size)], part.at[pl.ds(i * size, size)]
        else:
            source, target = whole.at[:, pl.ds(start, size)], part.at[:, pl.ds(i * size, size)]
        ins.append(pltpu.make_async_copy(source, buf.at[i], in_sems.at[i]))
        outs.append(pltpu.make_async_copy(buf.at[i], target, out_sems.at[i]))
    for copy in ins:
        copy.start()
    for before, after in zip(ins, outs):
        before.wait()
        after.start()
    for copy in outs:
        copy.wait()


def others_half(whole, plan, chips, by_rows):
    shape = (whole.shape[0] // 2, whole.shape[1]) if by_rows else (whole.shape[0], whole.shape[1] // 2)
    block = (shape[0] // chips, shape[1]) if by_rows else (shape[0], shape[1] // chips)
    anywhere = pl.BlockSpec(memory_space=pl.ANY)
    return pl.pallas_call(
        functools.partial(split_kernel, chips, by_rows),
        in_specs=[pl.BlockSpec(memory_space=pltpu.SMEM), anywhere],
        out_specs=anywhere,
        out_shape=jax.ShapeDtypeStruct(shape, whole.dtype),
        scratch_shapes=[
            pltpu.VMEM((chips,) + block, whole.dtype),
            pltpu.SemaphoreType.DMA((chips,)),
            pltpu.SemaphoreType.DMA((chips,)),
        ],
        cost_estimate=pl.CostEstimate(flops=0, bytes_accessed=2 * whole.size, transcendentals=0),
        compiler_params=pltpu.CompilerParams(vmem_limit_bytes=VMEM_LIMIT),
    )(plan, whole)


def query_kernel(bases, first, far, with_total, plan_ref, *refs):
    sides = len(far)
    count = sum(len(group) for group in bases)
    blocks = refs[:count]
    weights = refs[count : count + sides]
    before = refs[count + sides : count + 2 * sides] if with_total else None
    totals, buf, sems = refs[-sides - 2 : -2], refs[-2], refs[-1]
    depth = buf.shape[1]
    core = plan_ref[plan_ref.shape[0] - 1]
    copies = []
    for i in range(len(bases)):
        for side in range(sides):
            block = plan_ref[first + i]
            block = block if far[side] else 2 * block + core
            rows = pl.ds(pl.multiple_of(block * depth, depth), depth)
            n = i * sides + side
            copies.append(pltpu.make_async_copy(weights[side].at[rows], buf.at[n], sems.at[n]))
    for copy in copies:
        copy.start()
    for side in range(sides):
        if with_total:
            totals[side][...] = before[side][...]
        else:
            totals[side][...] = jnp.zeros_like(totals[side])
    at = 0
    for i, group in enumerate(bases):
        for side in range(sides):
            n = i * sides + side
            copies[n].wait()
            for g, base in enumerate(group):
                rows = pl.ds(base, blocks[at + g].shape[0])
                totals[side][rows, :] += jnp.dot(
                    blocks[at + g][...], buf[n], preferred_element_type=f32
                )
        at += len(group)


def query_terms(totals, groups, w_own, w_far, plan, first):
    blocks = [block for group in groups for block, _ in group]
    bases = [[base for _, base in group] for group in groups]
    depth = blocks[0].shape[1]
    rows = max(base + block.shape[0] for group in groups for block, base in group)
    weights = [w for w in (w_own, w_far) if w is not None]
    far = [w is w_far for w in weights]
    width = weights[0].shape[1]
    sides = len(weights)
    totals = list(totals) if totals is not None else []
    vmem = pl.BlockSpec(memory_space=pltpu.VMEM)
    return pl.pallas_call(
        functools.partial(query_kernel, bases, first, far, bool(totals)),
        in_specs=[pl.BlockSpec(memory_space=pltpu.SMEM)]
        + [vmem] * len(blocks)
        + [pl.BlockSpec(memory_space=pl.ANY)] * sides
        + [vmem] * len(totals),
        out_specs=[vmem] * sides,
        out_shape=[jax.ShapeDtypeStruct((rows, width), f32)] * sides,
        scratch_shapes=[
            pltpu.VMEM((sides * len(groups), depth, width), bf16),
            pltpu.SemaphoreType.DMA((sides * len(groups),)),
        ],
        cost_estimate=pl.CostEstimate(
            flops=2 * sides * sum(block.size for block in blocks) * width,
            bytes_accessed=2 * sides * len(groups) * depth * width
            + 2 * sum(block.size for block in blocks),
            transcendentals=0,
        ),
        compiler_params=pltpu.CompilerParams(vmem_limit_bytes=VMEM_LIMIT),
    )(plan, *blocks, *weights, *totals)


def out_kernel(first, amount, parts, plan_ref, own, far, w_own, w_far, *refs):
    outs, buf, sems = refs[:-2], refs[-2], refs[-1]
    width = buf.shape[2]
    core = plan_ref[plan_ref.shape[0] - 1]
    copies = []
    for i in range(amount):
        block = plan_ref[first + i]
        for side, weights in enumerate((w_own, w_far)):
            column = block if side else 2 * block + core
            columns = pl.ds(pl.multiple_of(column * width, width), width)
            n = 2 * i + side
            copies.append(pltpu.make_async_copy(weights.at[:, columns], buf.at[n], sems.at[n]))
    for copy in copies:
        copy.start()
    for i in range(amount):
        copies[2 * i].wait()
        value = jnp.dot(own[...], buf[2 * i], preferred_element_type=f32)
        copies[2 * i + 1].wait()
        value = value + jnp.dot(far[...], buf[2 * i + 1], preferred_element_type=f32)
        rows = value.shape[0] // parts
        for p in range(parts):
            target = outs[i * parts + p]
            target[...] = value[p * rows : (p + 1) * rows].astype(target.dtype)


def out_terms(own, far, w_own, w_far, plan, first, amount, width, kind, parts=1):
    rows, depth = own.shape
    vmem = pl.BlockSpec(memory_space=pltpu.VMEM)
    anywhere = pl.BlockSpec(memory_space=pl.ANY)
    return pl.pallas_call(
        functools.partial(out_kernel, first, amount, parts),
        in_specs=[pl.BlockSpec(memory_space=pltpu.SMEM), vmem, vmem, anywhere, anywhere],
        out_specs=[vmem] * (amount * parts),
        out_shape=[jax.ShapeDtypeStruct((rows // parts, width), kind)] * (amount * parts),
        scratch_shapes=[
            pltpu.VMEM((2 * amount, depth, width), bf16),
            pltpu.SemaphoreType.DMA((2 * amount,)),
        ],
        cost_estimate=pl.CostEstimate(
            flops=4 * rows * depth * width * amount,
            bytes_accessed=4 * depth * width * amount + 4 * rows * width * amount,
            transcendentals=0,
        ),
        compiler_params=pltpu.CompilerParams(vmem_limit_bytes=VMEM_LIMIT),
    )(plan, own, far, w_own, w_far)


def attend_kernel(
    source_ref, row_ref, length_ref,
    q_ref, cos_ref, sin_ref, new_ref, prefix_own, prefix_far, suffix_own, suffix_far,
    out_ref, prefix_buf, page_buf, q_buf, o_buf, prefix_sem, page_sem,
):
    prompts = prefix_buf.shape[0]
    devices, rows, width = q_ref.shape
    heads_here = width // HD
    per_kv = devices // KV
    page = page_buf.shape[3]
    group_rows = per_kv * heads_here * HALF

    def prefix_copies(j):
        return [
            pltpu.make_async_copy(prefix_own.at[0, j], prefix_buf.at[j, 0], prefix_sem.at[j, 0]),
            pltpu.make_async_copy(prefix_far.at[0, j], prefix_buf.at[j, 1], prefix_sem.at[j, 1]),
        ]

    def fetch(j):
        for copy in prefix_copies(j):
            copy.start()
        for b in range(HALF):
            r = j * HALF + b

            @pl.when(source_ref[r] == 0)
            def _():
                pltpu.make_async_copy(
                    suffix_own.at[row_ref[r]], page_buf.at[r], page_sem.at[r]
                ).start()

            @pl.when(source_ref[r] != 0)
            def _():
                pltpu.make_async_copy(
                    suffix_far.at[row_ref[r]], page_buf.at[r], page_sem.at[r]
                ).start()

    fetch(0)
    q_buf[...] = q_ref[...].astype(f32)
    row_beam = lax.broadcasted_iota(jnp.int32, (group_rows, page), 0) % HALF
    position = lax.broadcasted_iota(jnp.int32, (group_rows, page), 1)
    nt = (((1,), (1,)), ((), ()))

    def spread(four):
        return jnp.concatenate([four] * (group_rows // HALF), axis=0)

    for j in range(prompts):
        beams = slice(j * HALF, (j + 1) * HALF)
        cosine = spread(cos_ref[beams, :])
        sines = spread(sin_ref[beams, :])
        for copy in prefix_copies(j):
            copy.wait()
        masks = []
        for b in range(HALF):
            r = j * HALF + b
            pltpu.make_async_copy(suffix_own.at[0], page_buf.at[r], page_sem.at[r]).wait()
            masks.append((row_beam == b) & (position < length_ref[r]))
        if j + 1 < prompts:
            fetch(j + 1)
        for k in range(KV):
            pieces = [
                q_buf[k * per_kv + t, beams, h * HD : (h + 1) * HD]
                for t in range(per_kv)
                for h in range(heads_here)
            ]
            query = jnp.concatenate(pieces, axis=0)
            turned = query * cosine + pltpu.roll(query, HD // 2, 1) * sines
            turned = (turned * HD ** (-0.5)).astype(bf16)
            keys = [prefix_buf[j, 0, 0, k], prefix_buf[j, 1, 0, k]]
            values = [prefix_buf[j, 0, 1, k], prefix_buf[j, 1, 1, k]]
            scores = [lax.dot_general(turned, key, nt, preferred_element_type=f32) for key in keys]
            for b in range(HALF):
                r = j * HALF + b
                raw = lax.dot_general(turned, page_buf[r, 0, k], nt, preferred_element_type=f32)
                scores.append(jnp.where(masks[b], raw, big_negative))
                values.append(page_buf[r, 1, k])
            new_key = spread(new_ref[beams, k * HD : (k + 1) * HD])
            new_value = spread(new_ref[beams, (KV + k) * HD : (KV + k + 1) * HD])
            new_score = jnp.sum(turned.astype(f32) * new_key, axis=1, keepdims=True)
            highest = new_score
            for score in scores:
                highest = jnp.maximum(highest, jnp.max(score, axis=1, keepdims=True))
            new_weight = jnp.exp(new_score - highest)
            weight_sum = new_weight
            weighted = new_weight.astype(bf16).astype(f32) * new_value
            for score, value in zip(scores, values):
                weight = jnp.exp(score - highest)
                weight_sum = weight_sum + jnp.sum(weight, axis=1, keepdims=True)
                weighted = weighted + jnp.dot(
                    weight.astype(bf16), value, preferred_element_type=f32
                )
            result = weighted / weight_sum
            for t in range(per_kv):
                for h in range(heads_here):
                    at = (t * heads_here + h) * HALF
                    o_buf[k * per_kv + t, beams, h * HD : (h + 1) * HD] = result[at : at + HALF]
    out_ref[...] = o_buf[...].astype(bf16)


def attend(queries, cosine, sines, new_rows, prefix_own, prefix_far, suffix_own, suffix_far,
           source, row, page_len):
    devices, rows, width = queries.shape
    prompts = rows // HALF
    part = prefix_own.shape[4]
    page = suffix_own.shape[3]
    vmem = pl.BlockSpec(memory_space=pltpu.VMEM)
    smem = pl.BlockSpec(memory_space=pltpu.SMEM)
    anywhere = pl.BlockSpec(memory_space=pl.ANY)
    keys = rows * (2 * part + page)
    return pl.pallas_call(
        attend_kernel,
        in_specs=[smem] * 3 + [vmem] * 4 + [anywhere] * 4,
        out_specs=vmem,
        out_shape=jax.ShapeDtypeStruct(queries.shape, bf16),
        scratch_shapes=[
            pltpu.VMEM((prompts, 2) + prefix_own.shape[2:], bf16),
            pltpu.VMEM(suffix_own.shape, bf16),
            pltpu.VMEM(queries.shape, f32),
            pltpu.VMEM(queries.shape, f32),
            pltpu.SemaphoreType.DMA((prompts, 2)),
            pltpu.SemaphoreType.DMA((rows,)),
        ],
        cost_estimate=pl.CostEstimate(
            flops=4 * keys * HEADS * HD,
            bytes_accessed=2 * prefix_own.size * 2 + 2 * suffix_own.size,
            transcendentals=keys * HEADS,
        ),
        compiler_params=pltpu.CompilerParams(vmem_limit_bytes=VMEM_LIMIT),
    )(source, row, page_len, queries, cosine, sines, new_rows,
      prefix_own, prefix_far, suffix_own, suffix_far)


def body(hidden, w_query, w_out, new_kv, prefix_kv, suffix_kv, parents, lengths):
    count = lax.axis_size("tensor")
    order = ring_chips(count // 2)
    chips = len(order)
    hops = chips // 2
    me = lax.axis_index("tensor")
    core = me % 2
    plan = lax.dynamic_index_in_dim(make_plan(order, hops), me, keepdims=False)

    onward, backward = along(order, 1), along(order, -1)
    to_core = [(t, t ^ 1) for t in range(count)]
    rows_all, depth = hidden.shape
    rows_here = new_kv.shape[0]
    prompts_here = rows_here // HALF
    prefix_len = 2 * prefix_kv.shape[4]

    def tables(far_len):
        own_len = lengths.reshape(prompts_here, HALF)
        far_len = far_len.reshape(prompts_here, HALF)
        parent = parents.reshape(prompts_here, HALF)
        slot = parent % HALF
        from_far = (parent // HALF) != core
        chosen = [
            jnp.sum(jnp.where(slot[..., None] == jnp.arange(HALF), table[:, None, :], 0), axis=-1)
            for table in (own_len, far_len)
        ]
        page_len = jnp.where(from_far, chosen[1], chosen[0]).reshape(rows_here)
        page_row = (jnp.arange(prompts_here, dtype=jnp.int32)[:, None] * HALF + slot).reshape(rows_here)
        source = from_far.astype(jnp.int32).reshape(rows_here)
        frequency = rope_base ** (-jnp.arange(HD // 2, dtype=f32) * 2.0 / HD)
        angles = (prefix_len + page_len).astype(f32)[:, None] * frequency
        cosine = jnp.cos(angles)
        sines = jnp.sin(angles)
        cosine = jnp.concatenate([cosine, cosine], axis=1)
        sines = jnp.concatenate([-sines, sines], axis=1)
        new_rows = new_kv.astype(f32).reshape(rows_here, 2 * KV * HD)
        return cosine, sines, new_rows, source, page_row, page_len

    cut = rows_all // 2
    a = b = hidden
    blocks = [[(hidden, 0)]]
    own_total = far_total = None
    own_done = far_done = 0
    for s in range(1, hops + 1):
        if s == hops:
            a, b = a[:cut], b[cut:]
        a, b = send(a, onward), send(b, backward)
        if s == 1:
            far_len = send(lengths, to_core)
            prefix_far = send(prefix_kv, to_core)
            wq_send = others_half(w_query, plan, chips, True)
            a, b, far_len, prefix_far, wq_send = tied(a, b, far_len, prefix_far, wq_send)
            wq_far = send(wq_send, to_core)
        else:
            beside = []
            fresh = blocks[own_done:]
            if s == 2:
                own_total = query_terms(None, fresh, w_query, None, plan, 0)
                wo_send = others_half(w_out, plan, chips, False)
                beside = [wo_send] + list(tables(far_len))
            elif s == 3:
                own_total = query_terms(own_total, fresh, w_query, None, plan, own_done)
                far_total = list(query_terms(None, blocks, None, wq_far, plan, 0))
                wo_send, suffix_in, far_total[0] = tied(wo_send, suffix_kv, far_total[0])
                wo_far = send(wo_send, to_core)
                suffix_far = send(suffix_in, to_core)
            else:
                own_total, far_total = query_terms(
                    own_total + far_total, fresh, w_query, wq_far, plan, own_done
                )
                own_total, far_total = [own_total], [far_total]
            far_total = far_total or []
            a, b, *beside = tied(a, b, *own_total, *far_total, *beside)
            own_total, beside = beside[:1], beside[1:]
            if s > 2:
                far_total, beside = beside[:1], beside[1:]
            if s == 2:
                wo_send, cosine, sines, new_rows, source, page_row, page_len = beside
            own_done = len(blocks)
        if s < hops:
            blocks += [[(a, 0)], [(b, 0)]]
        else:
            blocks.append([(a, 0), (b, cut)])
    own_total, far_total = query_terms(
        own_total + far_total, blocks[own_done:], w_query, wq_far, plan, own_done
    )
    query = own_total + send(far_total, to_core)
    query = query.astype(bf16).reshape(count, rows_here, -1)

    query, suffix_far, wo_far = tied(query, suffix_far, wo_far)
    queries = lax.all_to_all(query, "tensor", split_axis=0, concat_axis=0, tiled=True)
    heads = attend(queries, cosine, sines, new_rows, prefix_kv, prefix_far, suffix_kv, suffix_far,
                   source, page_row, page_len)
    heads = lax.all_to_all(heads, "tensor", split_axis=0, concat_axis=0, tiled=True)
    own = heads.reshape(rows_all, -1)
    far = send(own, to_core)

    width = w_out.shape[1] // count

    def out(first, amount, kind, parts=1):
        return out_terms(own, far, w_out, wo_far, plan, chips + first, amount, width, kind, parts)

    up, down = tied(*out(0, 1, bf16, 2))
    a, b = send(up, onward), send(down, backward)
    for s in range(hops - 1, 0, -1):
        up, down = out(1 + 2 * (hops - 1 - s), 2, f32)
        a, b, up, down = tied(a, b, up, down)
        a, b = a.astype(f32), b.astype(f32)
        if s == hops - 1:
            up = jnp.concatenate([up[:cut] + a, up[cut:]], axis=0)
            down = jnp.concatenate([down[:cut], down[cut:] + b], axis=0)
        else:
            up, down = up + a, down + b
        a, b = tied(up.astype(bf16), down.astype(bf16))
        a, b = send(a, onward), send(b, backward)
    [own_term] = out(chips - 1, 1, f32)
    a, b, own_term = tied(a, b, own_term)
    return (own_term + a.astype(f32) + b.astype(f32)).astype(bf16)


def solution(mesh):
    return jax.shard_map(
        body,
        mesh=mesh,
        in_specs=(
            P("groups", "tensor"),
            P(None, "tensor"),
            P("tensor", None),
            P(("groups", "tensor"), None, None, None),
            P(("groups", "tensor"), None, None, None, None, None),
            P(("groups", "tensor"), None, None, None, None),
            P(("groups", "tensor")),
            P(("groups", "tensor")),
        ),
        out_specs=P("groups", "tensor"),
        check_vma=False,
    )
```

time: 228 us -> 143 us (0.63)
  waiting for transfers between devices: 118 us -> 38.1 us
  Pallas kernels: 0 us -> 53.9 us
  matrix products: 29.8 us -> 0 us
  local copies, waits for them, and re-layouts: 24.4 us -> 2.38 us
  other arithmetic: 24.1 us -> 2.71 us
  starting transfers between devices: 4.64 us -> 18.5 us
  blocking collectives: 12.8 us -> 26.6 us
  between operations: 13.6 us -> 0.32 us
    reduce_scatter x1 -> x0, waiting for transfers between devices: 83.7 us -> none  [body(): lax.psum_scatter(projected.astype(jnp.bfloat16), 'tensor', scatter_dimens...]
    pallas_call x0 -> x13, Pallas kernels: none -> 53.9 us  [the longest x5 15.7 us: out_terms(): pl.pallas_call(functools.partial(out_kernel, first, amount, parts), in_sp...]
    ppermute x3 -> x23, waiting for transfers between devices: 6.88 us -> 38.1 us  [send(): return lax.ppermute(block, 'tensor', route)]
    dot_general x7 -> x0, matrix products: 29.8 us -> none  [the longest x1 11.9 us: body(): projected = jnp.dot(heads_view, w_out, preferred_element_type=jnp.float32)]
    all_gather x1 -> x0, waiting for transfers between devices: 22.6 us -> none  [body(): lax.all_gather(hidden, 'tensor', axis=1, tiled=True)]
    ppermute x3 -> x23, starting transfers between devices: 1.03 us -> 18.5 us  [send(): return lax.ppermute(block, 'tensor', route)]
    gather x5 -> x0, local copies, waits for them, and re-layouts: 15.9 us -> none  [the longest x2 15 us: body(): jnp.take_along_axis(pages_all, own_par[:, :, None, None, None, None], axi...]
    select_n x4 -> x1, other arithmetic: 15 us -> 0.01 us  [tables(): slot = parent % HALF]
  transfers between devices with their start and end apart: 6 -> 23, of which waited for: 5 -> 18; matrix products, arithmetic and copies ran while one was open for 19% -> 2% of each run, Pallas kernels for 0% -> 27%
where the time goes in v1:
time: 143 us; the launch traced here: 142 us
  Pallas kernels  53.9 us (38%)
  waiting for transfers between devices  38.1 us (27%)
  blocking collectives  26.6 us (19%)
  starting transfers between devices  18.5 us (13%)
  other arithmetic  2.71 us (2%)
  local copies, waits for them, and re-layouts  2.38 us (2%)
    ppermute x23, waiting for transfers between devices, send(): return lax.ppermute(block, 'tensor', route)  38.1 us
    ppermute x23, starting transfers between devices, send(): return lax.ppermute(block, 'tensor', route)  18.5 us
    pallas_call x5, Pallas kernels, out_terms(): pl.pallas_call(functools.partial(out_kernel, first, amount, parts), in_sp...  15.7 us
    pallas_call x5, Pallas kernels, query_terms(): pl.pallas_call(functools.partial(query_kernel, bases, first, far, bool(to...  15 us
    pallas_call x2, Pallas kernels, others_half(): pl.pallas_call(functools.partial(split_kernel, chips, by_rows), in_specs=...  14.2 us
    all_to_all x1, blocking collectives, body(): lax.all_to_all(query, 'tensor', split_axis=0, concat_axis=0, tiled=True)  13.8 us
    all_to_all x1, blocking collectives, body(): lax.all_to_all(heads, 'tensor', split_axis=0, concat_axis=0, tiled=True)  12.8 us
    pallas_call x1, Pallas kernels, attend(): pl.pallas_call(attend_kernel, in_specs=[smem] * 3 + [vmem] * 4 + [anywher...  9.07 us
  transfers between devices with their start and end apart: 23, of which 18 were waited for; matrix products, arithmetic and copies ran while one was open for 2% of the time, Pallas kernels for 27%

profile of v1, /device:TPU:0, one launch (start us, length us, event | category | flops | bytes accessed | tf_op | source)
XLA Modules:
  0.0 142.5 jit_solution(4284188331927016829)
XLA Ops:
  0.5 2.6 %collective-permute-start = (bf16[192,1024]{1,0:T(8,128)(2,1)}, bf16[192,1024]{1,0:T(8,128)(2,1)S(1)}, u32[]{:S(2)}, u32[]{:S(2)}) collective-permute-start(bf16[192,1024]{1,0:T(8,128)(2,1)} %refs_0_.3), channel_id=1, source_target_pairs={{0,4},{1,5},{4,8},{5,9},{8,12},{9,13},{12,14},{13,15},{14,10},{15,... | collective-permute-start | bytes 1179656 | tf_op jit(solution)/shard_map/ppermute | solution.py:31
  4.0 7.1 %shard_map.91 = bf16[8192,512]{1,0:T(8,128)(2,1)} custom-call(s32[17]{0:T(128)S(1)} %dynamic-slice_bitcast_fusion.plan_ref, bf16[16384,512]{1,0:T(8,128)(2,1)} %refs_2_.5), custom_call_target="tpu_custom_call" | custom-call | bytes 16777216 | tf_op jit(solution)/shard_map/pallas_call | solution.py:83
  11.1 1.9 %collective-permute-done.refs_1_ = bf16[192,1024]{1,0:T(8,128)(2,1)S(1)} collective-permute-done((bf16[192,1024]{1,0:T(8,128)(2,1)}, bf16[192,1024]{1,0:T(8,128)(2,1)S(1)}, u32[]{:S(2)}, u32[]{:S(2)}) %collective-permute-start) | collective-permute-done | bytes 393248 | tf_op jit(solution)/shard_map/ppermute | solution.py:31
  14.7 7.1 %shard_map.93 = bf16[512,8192]{1,0:T(8,128)(2,1)} custom-call(s32[17]{0:T(128)S(1)} %dynamic-slice_bitcast_fusion.plan_ref, bf16[512,16384]{1,0:T(8,128)(2,1)} %w_own.9), custom_call_target="tpu_custom_call" | custom-call | bytes 16777216 | tf_op jit(solution)/shard_map/pallas_call | solution.py:83
  24.6 2.8 %shard_map.92.refs_3_ = f32[192,512]{1,0:T(8,128)S(1)} custom-call(s32[17]{0:T(128)S(1)} %dynamic-slice_bitcast_fusion.plan_ref, bf16[192,1024]{1,0:T(8,128)(2,1)S(1)} %copy-done.1, bf16[192,1024]{1,0:T(8,128)(2,1)S(1)} %collective-permute-done.refs_1_, bf16[192,1024]{1,0:T(8,128)(2,1)S(1)} %collective-permute-done.1.refs_2_, bf16[16384,512]{1,0:T(8,128)(2,1)} %refs_2_.5), custom_call_target="tpu_custom_call" | custom-call | flops 603979776 | bytes 4325376 | tf_op jit(solution)/shard_map/pallas_call | solution.py:146
  27.6 6.5 %collective-permute-done.4.refs_0_.refs_3_ = bf16[192,1024]{1,0:T(8,128)(2,1)S(1)} collective-permute-done((bf16[192,1024]{1,0:T(8,128)(2,1)S(1)}, bf16[192,1024]{1,0:T(8,128)(2,1)S(1)}, u32[]{:S(2)}, u32[]{:S(2)}) %collective-permute-start.4) | collective-permute-done | bytes 393248 | tf_op jit(solution)/shard_map/ppermute | solution.py:31
  35.4 3.5 %shard_map.95.refs_5_ = f32[192,512]{1,0:T(8,128)S(1)} custom-call(s32[17]{0:T(128)S(1)} %dynamic-slice_bitcast_fusion.plan_ref, bf16[192,1024]{1,0:T(8,128)(2,1)S(1)} %copy-done.1, bf16[192,1024]{1,0:T(8,128)(2,1)S(1)} %collective-permute-done.refs_1_, bf16[192,1024]{1,0:T(8,128)(2,1)S(1)} %collective-permute-done.1.refs_2_, ...), custom_call_target="tpu_custom_call" | custom-call | flops 1006632960 | bytes 7208960 | tf_op jit(solution)/shard_map/pallas_call | solution.py:146
  41.4 2.5 %shard_map.94.refs_4_ = f32[192,512]{1,0:T(8,128)S(1)} custom-call(s32[17]{0:T(128)S(1)} %dynamic-slice_bitcast_fusion.plan_ref, bf16[192,1024]{1,0:T(8,128)(2,1)S(1)} %collective-permute-done.4.refs_0_.refs_3_, bf16[192,1024]{1,0:T(8,128)(2,1)S(1)} %collective-permute-done.5.refs_1_.refs_4_, bf16[16384,512]{1,0:T(8,128)(2,1)} %refs_2_.5, ...), custom_call_target="tpu_custom_call" | custom-call | flops 402653184 | bytes 2883584 | tf_op jit(solution)/shard_map/pallas_call | solution.py:146
  43.9 6.6 %collective-permute-done.6.refs_0_ = bf16[192,1024]{1,0:T(8,128)(2,1)S(1)} collective-permute-done((bf16[192,1024]{1,0:T(8,128)(2,1)S(1)}, bf16[192,1024]{1,0:T(8,128)(2,1)S(1)}, u32[]{:S(2)}, u32[]{:S(2)}) %collective-permute-start.6) | collective-permute-done | bytes 393248 | tf_op jit(solution)/shard_map/ppermute | solution.py:31
  54.0 3.2 %shard_map.96 = (f32[192,512]{1,0:T(8,128)S(1)}, f32[192,512]{1,0:T(8,128)S(1)}) custom-call(s32[17]{0:T(128)S(1)} %dynamic-slice_bitcast_fusion.plan_ref, bf16[192,1024]{1,0:T(8,128)(2,1)S(1)} %collective-permute-done.6.refs_0_, bf16[192,1024]{1,0:T(8,128)(2,1)S(1)} %collective-permute-done.7.refs_1_, bf16[16384,512]{1,0:T(8,128)(2,1)} %refs_2_.5, ...), custom_call_target="tpu_custom_call" | custom-call | flops 805306368 | bytes 4980736 | tf_op jit(solution)/shard_map/pallas_call | solution.py:146
  58.1 3.0 %shard_map.97 = (f32[192,512]{1,0:T(8,128)S(1)}, f32[192,512]{1,0:T(8,128)S(1)}) custom-call(s32[17]{0:T(128)S(1)} %dynamic-slice_bitcast_fusion.plan_ref, bf16[96,1024]{1,0:T(8,128)(2,1)S(1)} %collective-permute-done.9.refs_0_, bf16[96,1024]{1,0:T(8,128)(2,1)S(1)} %collective-permute-done.10.refs_1_, bf16[16384,512]{1,0:T(8,128)(2,1)} %refs_2_.5, ...), custom_call_target="tpu_custom_call" | custom-call | flops 402653184 | bytes 2490368 | tf_op jit(solution)/shard_map/pallas_call | solution.py:146
  61.2 1.7 %collective-permute-done.11 = f32[192,512]{1,0:T(8,128)S(1)} collective-permute-done((f32[192,512]{1,0:T(8,128)S(1)}, f32[192,512]{1,0:T(8,128)S(1)}, u32[]{:S(2)}, u32[]{:S(2)}) %collective-permute-start.11) | collective-permute-done | bytes 393248 | tf_op jit(solution)/shard_map/ppermute | solution.py:31
  64.6 13.8 %all_to_all.10.q_ref = bf16[16,12,512]{2,1,0:T(8,128)(2,1)S(1)} all-to-all(bf16[16,12,512]{2,1,0:T(8,128)(2,1)S(1)} %reshape.59), channel_id=1, replica_groups=mesh['groups'=2,'tensor'=16] {'tensor'}, dimensions={0} | all-to-all | bytes 393216 | tf_op jit(solution)/shard_map/all_to_all | solution.py:436
  78.4 9.1 %shard_map.98 = bf16[16,12,512]{2,1,0:T(8,128)(2,1)S(1)} custom-call(s32[12]{0:T(128)S(1)} %get-tuple-element.70.source_ref, s32[12]{0:T(128)S(1)} %fusion.2.row_ref, s32[12]{0:T(128)S(1)} %get-tuple-element.72.length_ref, bf16[16,12,512]{2,1,0:T(8,128)(2,1)S(1)} %all_to_all.10.q_ref, f32[12,128]{1,0:T(8,128)S(1)} %get-tuple-element.94.cos_ref, ...), custom_call_target="tpu_custom_call" | custom-call | flops 503316480 | bytes 12582912 | tf_op jit(solution)/shard_map/pallas_call | solution.py:323
  87.4 12.8 %all_to_all.11 = bf16[16,12,512]{2,1,0:T(8,128)(2,1)S(1)} all-to-all(bf16[16,12,512]{2,1,0:T(8,128)(2,1)S(1)} %shard_map.98), channel_id=1, replica_groups=mesh['groups'=2,'tensor'=16] {'tensor'}, dimensions={0} | all-to-all | bytes 393216 | tf_op jit(solution)/shard_map/all_to_all | solution.py:439
  101.8 2.7 %shard_map.99 = (bf16[96,1024]{1,0:T(8,128)(2,1)S(1)}, bf16[96,1024]{1,0:T(8,128)(2,1)S(1)}) custom-call(s32[17]{0:T(128)S(1)} %dynamic-slice_bitcast_fusion.plan_ref, bf16[192,512]{1,0:T(8,128)(2,1)S(1)} %reshape.60.own, bf16[192,512]{1,0:T(8,128)(2,1)S(1)} %collective-permute-done.14.far, bf16[512,16384]{1,0:T(8,128)(2,1)} %w_own.9, ...), custom_call_target="tpu_custom_call" | custom-call | flops 402653184 | bytes 2883584 | tf_op jit(solution)/shard_map/pallas_call | solution.py:197
  104.9 1.7 %collective-permute-start.16 = (bf16[96,1024]{1,0:T(8,128)(2,1)S(1)}, bf16[96,1024]{1,0:T(8,128)(2,1)S(1)}, u32[]{:S(2)}, u32[]{:S(2)}) collective-permute-start(bf16[96,1024]{1,0:T(8,128)(2,1)S(1)} %get-tuple-element.101), channel_id=1, source_target_pairs={{0,2},{1,3},{4,0},{5,1},{8,4},{9,5},{12,8},{13,9},{14,12},{15,13},... | collective-permute-start | bytes 589832 | tf_op jit(solution)/shard_map/ppermute | solution.py:31
  106.6 3.4 %shard_map.100 = (f32[192,1024]{1,0:T(8,128)S(1)}, f32[192,1024]{1,0:T(8,128)S(1)}) custom-call(s32[17]{0:T(128)S(1)} %dynamic-slice_bitcast_fusion.plan_ref, bf16[192,512]{1,0:T(8,128)(2,1)S(1)} %reshape.60.own, bf16[192,512]{1,0:T(8,128)(2,1)S(1)} %collective-permute-done.14.far, bf16[512,16384]{1,0:T(8,128)(2,1)} %w_own.9, ...), custom_call_target="tpu_custom_call" | custom-call | flops 805306368 | bytes 5767168 | tf_op jit(solution)/shard_map/pallas_call | solution.py:197
  114.1 3.4 %shard_map.101 = (f32[192,1024]{1,0:T(8,128)S(1)}, f32[192,1024]{1,0:T(8,128)S(1)}) custom-call(s32[17]{0:T(128)S(1)} %dynamic-slice_bitcast_fusion.plan_ref, bf16[192,512]{1,0:T(8,128)(2,1)S(1)} %reshape.60.own, bf16[192,512]{1,0:T(8,128)(2,1)S(1)} %collective-permute-done.14.far, bf16[512,16384]{1,0:T(8,128)(2,1)} %w_own.9, ...), custom_call_target="tpu_custom_call" | custom-call | flops 805306368 | bytes 5767168 | tf_op jit(solution)/shard_map/pallas_call | solution.py:197
  117.6 4.8 %collective-permute-done.17 = bf16[192,1024]{1,0:T(8,128)(2,1)S(1)} collective-permute-done((bf16[192,1024]{1,0:T(8,128)(2,1)S(1)}, bf16[192,1024]{1,0:T(8,128)(2,1)S(1)}, u32[]{:S(2)}, u32[]{:S(2)}) %collective-permute-start.17) | collective-permute-done | bytes 393248 | tf_op jit(solution)/shard_map/ppermute | solution.py:31
  125.2 3.4 %shard_map.102 = (f32[192,1024]{1,0:T(8,128)S(1)}, f32[192,1024]{1,0:T(8,128)S(1)}) custom-call(s32[17]{0:T(128)S(1)} %dynamic-slice_bitcast_fusion.plan_ref, bf16[192,512]{1,0:T(8,128)(2,1)S(1)} %reshape.60.own, bf16[192,512]{1,0:T(8,128)(2,1)S(1)} %collective-permute-done.14.far, bf16[512,16384]{1,0:T(8,128)(2,1)} %w_own.9, ...), custom_call_target="tpu_custom_call" | custom-call | flops 805306368 | bytes 5767168 | tf_op jit(solution)/shard_map/pallas_call | solution.py:197
  128.6 3.4 %collective-permute-done.19 = bf16[192,1024]{1,0:T(8,128)(2,1)S(1)} collective-permute-done((bf16[192,1024]{1,0:T(8,128)(2,1)S(1)}, bf16[192,1024]{1,0:T(8,128)(2,1)S(1)}, u32[]{:S(2)}, u32[]{:S(2)}) %collective-permute-start.19) | collective-permute-done | bytes 393248 | tf_op jit(solution)/shard_map/ppermute | solution.py:31
  135.2 2.7 %shard_map.103 = f32[192,1024]{1,0:T(8,128)S(1)} custom-call(s32[17]{0:T(128)S(1)} %dynamic-slice_bitcast_fusion.plan_ref, bf16[192,512]{1,0:T(8,128)(2,1)S(1)} %reshape.60.own, bf16[192,512]{1,0:T(8,128)(2,1)S(1)} %collective-permute-done.14.far, bf16[512,16384]{1,0:T(8,128)(2,1)} %w_own.9, bf16[512,8192]{1,0:T(8,128)(2,1)} %collective-permute-done.13.w_far), custom_call_target="tpu_custom_call" | custom-call | flops 402653184 | bytes 2883584 | tf_op jit(solution)/shard_map/pallas_call | solution.py:197
  137.9 3.1 %collective-permute-done.21 = bf16[192,1024]{1,0:T(8,128)(2,1)S(1)} collective-permute-done((bf16[192,1024]{1,0:T(8,128)(2,1)S(1)}, bf16[192,1024]{1,0:T(8,128)(2,1)S(1)}, u32[]{:S(2)}, u32[]{:S(2)}) %collective-permute-start.21) | collective-permute-done | bytes 393248 | tf_op jit(solution)/shard_map/ppermute | solution.py:31
  (81 shorter events, 29.5 us)
Async XLA Ops:
  0.0 14.5 %collective-permute-start.3 = (bf16[1,3,2,4,512,128]{5,4,3,2,1,0:T(8,128)(2,1)}, bf16[1,3,2,4,512,128]{5,4,3,2,1,0:T(8,128)(2,1)}, u32[]{:S(2)}, u32[]{:S(2)}) collective-permute-start(bf16[1,3,2,4,512,128]{5,4,3,2,1,0:T(8,128)(2,1)} %prefix_own.1), channel_id=1, source_target_pairs={{0,1},{1,0},{2,3},{3,2},{4,5},{5,4},{6,7},{7,6},{8,9},{9,8},{10,11... | collective-permute-start | bytes 9437192 | tf_op jit(solution)/shard_map/ppermute | solution.py:31
  0.5 12.5 %collective-permute-start = (bf16[192,1024]{1,0:T(8,128)(2,1)}, bf16[192,1024]{1,0:T(8,128)(2,1)S(1)}, u32[]{:S(2)}, u32[]{:S(2)}) collective-permute-start(bf16[192,1024]{1,0:T(8,128)(2,1)} %refs_0_.3), channel_id=1, source_target_pairs={{0,4},{1,5},{4,8},{5,9},{8,12},{9,13},{12,14},{13,15},{14,10},{15,... | collective-permute-start | bytes 1179656 | tf_op jit(solution)/shard_map/ppermute | solution.py:31
  3.0 11.5 %collective-permute-start.1 = (bf16[192,1024]{1,0:T(8,128)(2,1)}, bf16[192,1024]{1,0:T(8,128)(2,1)S(1)}, u32[]{:S(2)}, u32[]{:S(2)}) collective-permute-start(bf16[192,1024]{1,0:T(8,128)(2,1)} %refs_0_.3), channel_id=1, source_target_pairs={{0,2},{1,3},{4,0},{5,1},{8,4},{9,5},{12,8},{13,9},{14,12},{15,13},... | collective-permute-start | bytes 1179656 | tf_op jit(solution)/shard_map/ppermute | solution.py:31
  3.0 8.0 %collective-permute-start.2 = (s32[12]{0:T(128)}, s32[12]{0:T(128)S(1)}, u32[]{:S(2)}, u32[]{:S(2)}) collective-permute-start(s32[12]{0:T(128)} %param.16), channel_id=1, source_target_pairs={{0,1},{1,0},{2,3},{3,2},{4,5},{5,4},{6,7},{7,6},{8,9},{9,8},{10,11... | collective-permute-start | bytes 152 | tf_op jit(solution)/shard_map/ppermute | solution.py:31
  14.5 20.9 %collective-permute-start.8 = (bf16[8192,512]{1,0:T(8,128)(2,1)}, bf16[8192,512]{1,0:T(8,128)(2,1)}, u32[]{:S(2)}, u32[]{:S(2)}) collective-permute-start(bf16[8192,512]{1,0:T(8,128)(2,1)} %shard_map.91), channel_id=1, source_target_pairs={{0,1},{1,0},{2,3},{3,2},{4,5},{5,4},{6,7},{7,6},{8,9},{9,8},{10,11... | collective-permute-start | bytes 25165832 | tf_op jit(solution)/shard_map/ppermute | solution.py:31
  22.5 11.5 %collective-permute-start.4 = (bf16[192,1024]{1,0:T(8,128)(2,1)S(1)}, bf16[192,1024]{1,0:T(8,128)(2,1)S(1)}, u32[]{:S(2)}, u32[]{:S(2)}) collective-permute-start(bf16[192,1024]{1,0:T(8,128)(2,1)S(1)} %collective-permute-done.refs_1_), channel_id=1, source_target_pairs={{0,4},{1,5},{4,8},{5,9},{8,12},{9,13},{12,14},{13,15},{14,10},{15,... | collective-permute-start | bytes 1179656 | tf_op jit(solution)/shard_map/ppermute | solution.py:31
  24.1 11.2 %collective-permute-start.5 = (bf16[192,1024]{1,0:T(8,128)(2,1)S(1)}, bf16[192,1024]{1,0:T(8,128)(2,1)S(1)}, u32[]{:S(2)}, u32[]{:S(2)}) collective-permute-start(bf16[192,1024]{1,0:T(8,128)(2,1)S(1)} %collective-permute-done.1.refs_2_), channel_id=1, source_target_pairs={{0,2},{1,3},{4,0},{5,1},{8,4},{9,5},{12,8},{13,9},{14,12},{15,13},... | collective-permute-start | bytes 1179656 | tf_op jit(solution)/shard_map/ppermute | solution.py:31
  38.8 25.8 %collective-permute-start.13 = (bf16[512,8192]{1,0:T(8,128)(2,1)}, bf16[512,8192]{1,0:T(8,128)(2,1)}, u32[]{:S(2)}, u32[]{:S(2)}) collective-permute-start(bf16[512,8192]{1,0:T(8,128)(2,1)} %shard_map.93), channel_id=1, source_target_pairs={{0,1},{1,0},{2,3},{3,2},{4,5},{5,4},{6,7},{7,6},{8,9},{9,8},{10,11... | collective-permute-start | bytes 25165832 | tf_op jit(solution)/shard_map/ppermute | solution.py:31
  38.9 25.7 %collective-permute-start.12 = (bf16[12,2,4,256,128]{4,3,2,1,0:T(8,128)(2,1)}, bf16[12,2,4,256,128]{4,3,2,1,0:T(8,128)(2,1)}, u32[]{:S(2)}, u32[]{:S(2)}) collective-permute-start(bf16[12,2,4,256,128]{4,3,2,1,0:T(8,128)(2,1)} %suffix_own.1), channel_id=1, source_target_pairs={{0,1},{1,0},{2,3},{3,2},{4,5},{5,4},{6,7},{7,6},{8,9},{9,8},{10,11... | collective-permute-start | bytes 18874376 | tf_op jit(solution)/shard_map/ppermute | solution.py:31
  39.4 11.1 %collective-permute-start.6 = (bf16[192,1024]{1,0:T(8,128)(2,1)S(1)}, bf16[192,1024]{1,0:T(8,128)(2,1)S(1)}, u32[]{:S(2)}, u32[]{:S(2)}) collective-permute-start(bf16[192,1024]{1,0:T(8,128)(2,1)S(1)} %collective-permute-done.4.refs_0_.refs_3_), channel_id=1, source_target_pairs={{0,4},{1,5},{4,8},{5,9},{8,12},{9,13},{12,14},{13,15},{14,10},{15,... | collective-permute-start | bytes 1179656 | tf_op jit(solution)/shard_map/ppermute | solution.py:31
  41.0 10.8 %collective-permute-start.7 = (bf16[192,1024]{1,0:T(8,128)(2,1)S(1)}, bf16[192,1024]{1,0:T(8,128)(2,1)S(1)}, u32[]{:S(2)}, u32[]{:S(2)}) collective-permute-start(bf16[192,1024]{1,0:T(8,128)(2,1)S(1)} %collective-permute-done.5.refs_1_.refs_4_), channel_id=1, source_target_pairs={{0,2},{1,3},{4,0},{5,1},{8,4},{9,5},{12,8},{13,9},{14,12},{15,13},... | collective-permute-start | bytes 1179656 | tf_op jit(solution)/shard_map/ppermute | solution.py:31
  51.8 5.8 %collective-permute-start.10 = (bf16[96,1024]{1,0:T(8,128)(2,1)S(1)}, bf16[96,1024]{1,0:T(8,128)(2,1)S(1)}, u32[]{:S(2)}, u32[]{:S(2)}) collective-permute-start(bf16[96,1024]{1,0:T(8,128)(2,1)S(1)} %slice.21), channel_id=1, source_target_pairs={{0,2},{1,3},{4,0},{5,1},{8,4},{9,5},{12,8},{13,9},{14,12},{15,13},... | collective-permute-start | bytes 589832 | tf_op jit(solution)/shard_map/ppermute | solution.py:31
  52.3 5.7 %collective-permute-start.9 = (bf16[96,1024]{1,0:T(8,128)(2,1)S(1)}, bf16[96,1024]{1,0:T(8,128)(2,1)S(1)}, u32[]{:S(2)}, u32[]{:S(2)}) collective-permute-start(bf16[96,1024]{1,0:T(8,128)(2,1)S(1)} %slice.20), channel_id=1, source_target_pairs={{0,4},{1,5},{4,8},{5,9},{8,12},{9,13},{12,14},{13,15},{14,10},{15,... | collective-permute-start | bytes 589832 | tf_op jit(solution)/shard_map/ppermute | solution.py:31
  58.1 20.3 %copy-start = (bf16[1,3,2,4,512,128]{5,4,3,2,1,0:T(8,128)(2,1)S(1)}, bf16[1,3,2,4,512,128]{5,4,3,2,1,0:T(8,128)(2,1)}, u32[]{:S(2)}) copy-start(bf16[1,3,2,4,512,128]{5,4,3,2,1,0:T(8,128)(2,1)} %prefix_own.1) | copy-start | bytes 9437188
  61.1 1.8 %collective-permute-start.11 = (f32[192,512]{1,0:T(8,128)S(1)}, f32[192,512]{1,0:T(8,128)S(1)}, u32[]{:S(2)}, u32[]{:S(2)}) collective-permute-start(f32[192,512]{1,0:T(8,128)S(1)} %get-tuple-element.90), channel_id=1, source_target_pairs={{0,1},{1,0},{2,3},{3,2},{4,5},{5,4},{6,7},{7,6},{8,9},{9,8},{10,11... | collective-permute-start | bytes 1179656 | tf_op jit(solution)/shard_map/ppermute | solution.py:31
  100.3 1.5 %collective-permute-start.14 = (bf16[192,512]{1,0:T(8,128)(2,1)S(1)}, bf16[192,512]{1,0:T(8,128)(2,1)S(1)}, u32[]{:S(2)}, u32[]{:S(2)}) collective-permute-start(bf16[192,512]{1,0:T(8,128)(2,1)S(1)} %reshape.60.own), channel_id=1, source_target_pairs={{0,1},{1,0},{2,3},{3,2},{4,5},{5,4},{6,7},{7,6},{8,9},{9,8},{10,11... | collective-permute-start | bytes 589832 | tf_op jit(solution)/shard_map/ppermute | solution.py:31
  104.5 7.0 %collective-permute-start.15 = (bf16[96,1024]{1,0:T(8,128)(2,1)S(1)}, bf16[96,1024]{1,0:T(8,128)(2,1)S(1)}, u32[]{:S(2)}, u32[]{:S(2)}) collective-permute-start(bf16[96,1024]{1,0:T(8,128)(2,1)S(1)} %get-tuple-element.100), channel_id=1, source_target_pairs={{0,4},{1,5},{4,8},{5,9},{8,12},{9,13},{12,14},{13,15},{14,10},{15,... | collective-permute-start | bytes 589832 | tf_op jit(solution)/shard_map/ppermute | solution.py:31
  104.9 6.9 %collective-permute-start.16 = (bf16[96,1024]{1,0:T(8,128)(2,1)S(1)}, bf16[96,1024]{1,0:T(8,128)(2,1)S(1)}, u32[]{:S(2)}, u32[]{:S(2)}) collective-permute-start(bf16[96,1024]{1,0:T(8,128)(2,1)S(1)} %get-tuple-element.101), channel_id=1, source_target_pairs={{0,2},{1,3},{4,0},{5,1},{8,4},{9,5},{12,8},{13,9},{14,12},{15,13},... | collective-permute-start | bytes 589832 | tf_op jit(solution)/shard_map/ppermute | solution.py:31
  112.1 10.3 %collective-permute-start.17 = (bf16[192,1024]{1,0:T(8,128)(2,1)S(1)}, bf16[192,1024]{1,0:T(8,128)(2,1)S(1)}, u32[]{:S(2)}, u32[]{:S(2)}) collective-permute-start(bf16[192,1024]{1,0:T(8,128)(2,1)S(1)} %pad_maximum_fusion), channel_id=1, source_target_pairs={{0,4},{1,5},{4,8},{5,9},{8,12},{9,13},{12,14},{13,15},{14,10},{15,... | collective-permute-start | bytes 1179656 | tf_op jit(solution)/shard_map/ppermute | solution.py:31
  113.2 9.7 %collective-permute-start.18 = (bf16[192,1024]{1,0:T(8,128)(2,1)S(1)}, bf16[192,1024]{1,0:T(8,128)(2,1)S(1)}, u32[]{:S(2)}, u32[]{:S(2)}) collective-permute-start(bf16[192,1024]{1,0:T(8,128)(2,1)S(1)} %pad_maximum_fusion.1), channel_id=1, source_target_pairs={{0,2},{1,3},{4,0},{5,1},{8,4},{9,5},{12,8},{13,9},{14,12},{15,13},... | collective-permute-start | bytes 1179656 | tf_op jit(solution)/shard_map/ppermute | solution.py:31
  123.1 8.9 %collective-permute-start.19 = (bf16[192,1024]{1,0:T(8,128)(2,1)S(1)}, bf16[192,1024]{1,0:T(8,128)(2,1)S(1)}, u32[]{:S(2)}, u32[]{:S(2)}) collective-permute-start(bf16[192,1024]{1,0:T(8,128)(2,1)S(1)} %add_convert_fusion.4), channel_id=1, source_target_pairs={{0,4},{1,5},{4,8},{5,9},{8,12},{9,13},{12,14},{13,15},{14,10},{15,... | collective-permute-start | bytes 1179656 | tf_op jit(solution)/shard_map/ppermute | solution.py:31
  124.1 8.8 %collective-permute-start.20 = (bf16[192,1024]{1,0:T(8,128)(2,1)S(1)}, bf16[192,1024]{1,0:T(8,128)(2,1)S(1)}, u32[]{:S(2)}, u32[]{:S(2)}) collective-permute-start(bf16[192,1024]{1,0:T(8,128)(2,1)S(1)} %add_convert_fusion.3), channel_id=1, source_target_pairs={{0,2},{1,3},{4,0},{5,1},{8,4},{9,5},{12,8},{13,9},{14,12},{15,13},... | collective-permute-start | bytes 1179656 | tf_op jit(solution)/shard_map/ppermute | solution.py:31
  133.1 7.9 %collective-permute-start.21 = (bf16[192,1024]{1,0:T(8,128)(2,1)S(1)}, bf16[192,1024]{1,0:T(8,128)(2,1)S(1)}, u32[]{:S(2)}, u32[]{:S(2)}) collective-permute-start(bf16[192,1024]{1,0:T(8,128)(2,1)S(1)} %add_convert_fusion.2), channel_id=1, source_target_pairs={{0,4},{1,5},{4,8},{5,9},{8,12},{9,13},{12,14},{13,15},{14,10},{15,... | collective-permute-start | bytes 1179656 | tf_op jit(solution)/shard_map/ppermute | solution.py:31
  133.8 7.8 %collective-permute-start.22 = (bf16[192,1024]{1,0:T(8,128)(2,1)S(1)}, bf16[192,1024]{1,0:T(8,128)(2,1)S(1)}, u32[]{:S(2)}, u32[]{:S(2)}) collective-permute-start(bf16[192,1024]{1,0:T(8,128)(2,1)S(1)} %add_convert_fusion.1), channel_id=1, source_target_pairs={{0,2},{1,3},{4,0},{5,1},{8,4},{9,5},{12,8},{13,9},{14,12},{15,13},... | collective-permute-start | bytes 1179656 | tf_op jit(solution)/shard_map/ppermute | solution.py:31
  (4 other events, 38.2 us)

commit v2 on v1

--- a/solution.py
+++ b/solution.py
@@ -19,6 +19,7 @@
 bf16 = jnp.bfloat16
 MIB = 1024 * 1024
 VMEM_LIMIT = 48 * MIB
+BESIDE = pl.CostEstimate(flops=1000, bytes_accessed=1000, transcendentals=0)
 
 
 def ring_chips(count):
@@ -90,18 +91,21 @@
             pltpu.SemaphoreType.DMA((chips,)),
             pltpu.SemaphoreType.DMA((chips,)),
         ],
-        cost_estimate=pl.CostEstimate(flops=0, bytes_accessed=2 * whole.size, transcendentals=0),
+        cost_estimate=BESIDE,
         compiler_params=pltpu.CompilerParams(vmem_limit_bytes=VMEM_LIMIT),
     )(plan, whole)
 
 
-def query_kernel(bases, first, far, with_total, plan_ref, *refs):
+def query_kernel(bases, first, far, with_total, closing, plan_ref, *refs):
     sides = len(far)
     count = sum(len(group) for group in bases)
     blocks = refs[:count]
     weights = refs[count : count + sides]
     before = refs[count + sides : count + 2 * sides] if with_total else None
-    totals, buf, sems = refs[-sides - 2 : -2], refs[-2], refs[-1]
+    if closing:
+        keep, give, buf, sems, *totals = refs[-4 - sides :]
+    else:
+        totals, buf, sems = refs[-sides - 2 : -2], refs[-2], refs[-1]
     depth = buf.shape[1]
     core = plan_ref[plan_ref.shape[0] - 1]
     copies = []
@@ -130,9 +134,30 @@
                     blocks[at + g][...], buf[n], preferred_element_type=f32
                 )
         at += len(group)
-
-
-def query_terms(totals, groups, w_own, w_far, plan, first):
+    if not closing:
+        return
+    chips = (plan_ref.shape[0] - 1) // 2
+    rows_here = totals[0].shape[0] // (2 * chips)
+    heads = totals[0].shape[1] // HD
+
+    def hand_out(side):
+        for chip in range(chips):
+            for to in range(2):
+                target = keep if to == side else give
+                rows = slice((2 * chip + to) * rows_here, (2 * chip + to + 1) * rows_here)
+                for half in range(2):
+                    source = totals[0 if half == side else 1]
+                    for h in range(heads):
+                        start = chip * rows_here * 2 * heads + half * heads + h
+                        target[pl.ds(start, rows_here, 2 * heads), :] = source[
+                            rows, h * HD : (h + 1) * HD
+                        ]
+
+    for side in range(2):
+        pl.when(core == side)(functools.partial(hand_out, side))
+
+
+def query_terms(totals, groups, w_own, w_far, plan, first, closing=False):
     blocks = [block for group in groups for block, _ in group]
     bases = [[base for _, base in group] for group in groups]
     depth = blocks[0].shape[1]
@@ -143,73 +168,96 @@
     sides = len(weights)
     totals = list(totals) if totals is not None else []
     vmem = pl.BlockSpec(memory_space=pltpu.VMEM)
+    shape = (rows * width // HD, HD) if closing else (rows, width)
     return pl.pallas_call(
-        functools.partial(query_kernel, bases, first, far, bool(totals)),
+        functools.partial(query_kernel, bases, first, far, bool(totals), closing),
         in_specs=[pl.BlockSpec(memory_space=pltpu.SMEM)]
         + [vmem] * len(blocks)
         + [pl.BlockSpec(memory_space=pl.ANY)] * sides
         + [vmem] * len(totals),
         out_specs=[vmem] * sides,
-        out_shape=[jax.ShapeDtypeStruct((rows, width), f32)] * sides,
+        out_shape=[jax.ShapeDtypeStruct(shape, f32)] * sides,
         scratch_shapes=[
             pltpu.VMEM((sides * len(groups), depth, width), bf16),
             pltpu.SemaphoreType.DMA((sides * len(groups),)),
-        ],
-        cost_estimate=pl.CostEstimate(
-            flops=2 * sides * sum(block.size for block in blocks) * width,
-            bytes_accessed=2 * sides * len(groups) * depth * width
-            + 2 * sum(block.size for block in blocks),
-            transcendentals=0,
-        ),
+        ]
+        + [pltpu.VMEM((rows, width), f32)] * (sides if closing else 0),
+        cost_estimate=BESIDE,
         compiler_params=pltpu.CompilerParams(vmem_limit_bytes=VMEM_LIMIT),
     )(plan, *blocks, *weights, *totals)
 
 
-def out_kernel(first, amount, parts, plan_ref, own, far, w_own, w_far, *refs):
-    outs, buf, sems = refs[:-2], refs[-2], refs[-1]
-    width = buf.shape[2]
+def out_kernel(first, amount, parts, opening, plan_ref, *refs):
     core = plan_ref[plan_ref.shape[0] - 1]
+    if opening:
+        mine, other, w_own, w_far = refs[:4]
+        outs, lhs, (buf, sems, mixed, flat) = refs[4:-5], refs[-5], refs[-4:]
+    else:
+        lhs, w_own, w_far = refs[:3]
+        outs, (buf, sems) = refs[3:-2], refs[-2:]
+    width = buf.shape[3]
     copies = []
     for i in range(amount):
         block = plan_ref[first + i]
         for side, weights in enumerate((w_own, w_far)):
             column = block if side else 2 * block + core
             columns = pl.ds(pl.multiple_of(column * width, width), width)
-            n = 2 * i + side
-            copies.append(pltpu.make_async_copy(weights.at[:, columns], buf.at[n], sems.at[n]))
+            owner = 1 - core if side else core
+            copies.append(
+                pltpu.make_async_copy(weights.at[:, columns], buf.at[i, owner], sems.at[2 * i + side])
+            )
     for copy in copies:
         copy.start()
+    if opening:
+        chips = (plan_ref.shape[0] - 1) // 2
+        rows_here = lhs.shape[0] // (2 * chips)
+        heads = lhs.shape[1] // HD
+        halves = [mine[...].astype(f32), other[...].astype(f32)]
+        for side in range(2):
+            mixed[...] = jnp.where(core == side, halves[0], halves[1])
+            for h in range(heads):
+                columns = slice(h * HD, (h + 1) * HD)
+                for chip in range(chips):
+                    rows = slice((2 * chip + side) * rows_here, (2 * chip + side + 1) * rows_here)
+                    start = chip * rows_here * heads + h
+                    flat[rows, columns] = mixed[pl.ds(start, rows_here, heads), :]
+        lhs[...] = flat[...].astype(bf16)
     for i in range(amount):
         copies[2 * i].wait()
-        value = jnp.dot(own[...], buf[2 * i], preferred_element_type=f32)
         copies[2 * i + 1].wait()
-        value = value + jnp.dot(far[...], buf[2 * i + 1], preferred_element_type=f32)
+        depth = buf.shape[2]
+        value = jnp.dot(lhs[:, :depth], buf[i, 0], preferred_element_type=f32)
+        value = value + jnp.dot(lhs[:, depth:], buf[i, 1], preferred_element_type=f32)
         rows = value.shape[0] // parts
         for p in range(parts):
             target = outs[i * parts + p]
             target[...] = value[p * rows : (p + 1) * rows].astype(target.dtype)
 
 
-def out_terms(own, far, w_own, w_far, plan, first, amount, width, kind, parts=1):
-    rows, depth = own.shape
+def out_terms(heads, w_own, w_far, plan, first, amount, width, kind, parts=1):
+    opening = isinstance(heads, tuple)
+    depth = w_own.shape[0]
+    rows = 2 * heads[0].size // (2 * depth) if opening else heads.shape[0]
     vmem = pl.BlockSpec(memory_space=pltpu.VMEM)
     anywhere = pl.BlockSpec(memory_space=pl.ANY)
+    args = list(heads) if opening else [heads]
+    shapes = [jax.ShapeDtypeStruct((rows // parts, width), kind)] * (amount * parts)
+    scratch = [
+        pltpu.VMEM((amount, 2, depth, width), bf16),
+        pltpu.SemaphoreType.DMA((2 * amount,)),
+    ]
+    if opening:
+        shapes.append(jax.ShapeDtypeStruct((rows, 2 * depth), bf16))
+        scratch += [pltpu.VMEM(heads[0].shape, f32), pltpu.VMEM((rows, 2 * depth), f32)]
     return pl.pallas_call(
-        functools.partial(out_kernel, first, amount, parts),
-        in_specs=[pl.BlockSpec(memory_space=pltpu.SMEM), vmem, vmem, anywhere, anywhere],
-        out_specs=[vmem] * (amount * parts),
-        out_shape=[jax.ShapeDtypeStruct((rows // parts, width), kind)] * (amount * parts),
-        scratch_shapes=[
-            pltpu.VMEM((2 * amount, depth, width), bf16),
-            pltpu.SemaphoreType.DMA((2 * amount,)),
-        ],
-        cost_estimate=pl.CostEstimate(
-            flops=4 * rows * depth * width * amount,
-            bytes_accessed=4 * depth * width * amount + 4 * rows * width * amount,
-            transcendentals=0,
-        ),
+        functools.partial(out_kernel, first, amount, parts, opening),
+        in_specs=[pl.BlockSpec(memory_space=pltpu.SMEM)] + [vmem] * len(args) + [anywhere] * 2,
+        out_specs=[vmem] * len(shapes),
+        out_shape=shapes,
+        scratch_shapes=scratch,
+        cost_estimate=BESIDE,
         compiler_params=pltpu.CompilerParams(vmem_limit_bytes=VMEM_LIMIT),
-    )(plan, own, far, w_own, w_far)
+    )(plan, *args, w_own, w_far)
 
 
 def attend_kernel(
@@ -218,11 +266,11 @@
     out_ref, prefix_buf, page_buf, q_buf, o_buf, prefix_sem, page_sem,
 ):
     prompts = prefix_buf.shape[0]
-    devices, rows, width = q_ref.shape
-    heads_here = width // HD
-    per_kv = devices // KV
+    chips = q_ref.shape[0]
+    heads_here = HEADS // chips
+    per_kv = chips // KV
     page = page_buf.shape[3]
-    group_rows = per_kv * heads_here * HALF
+    beam_rows = per_kv * heads_here
 
     def prefix_copies(j):
         return [
@@ -250,69 +298,100 @@
 
     fetch(0)
     q_buf[...] = q_ref[...].astype(f32)
-    row_beam = lax.broadcasted_iota(jnp.int32, (group_rows, page), 0) % HALF
-    position = lax.broadcasted_iota(jnp.int32, (group_rows, page), 1)
+    position = lax.broadcasted_iota(jnp.int32, (beam_rows, page), 1)
     nt = (((1,), (1,)), ((), ()))
 
-    def spread(four):
-        return jnp.concatenate([four] * (group_rows // HALF), axis=0)
-
     for j in range(prompts):
-        beams = slice(j * HALF, (j + 1) * HALF)
-        cosine = spread(cos_ref[beams, :])
-        sines = spread(sin_ref[beams, :])
         for copy in prefix_copies(j):
             copy.wait()
-        masks = []
         for b in range(HALF):
             r = j * HALF + b
             pltpu.make_async_copy(suffix_own.at[0], page_buf.at[r], page_sem.at[r]).wait()
-            masks.append((row_beam == b) & (position < length_ref[r]))
         if j + 1 < prompts:
             fetch(j + 1)
+
+        def spread(ref, columns):
+            return jnp.concatenate(
+                [
+                    jnp.broadcast_to(ref[r : r + 1, columns], (beam_rows, HD))
+                    for r in range(j * HALF, (j + 1) * HALF)
+                ],
+                axis=0,
+            )
+
+        everything = slice(0, HD)
+        cosine = spread(cos_ref, everything)
+        sines = spread(sin_ref, everything)
+        masks = [position < length_ref[j * HALF + b] for b in range(HALF)]
         for k in range(KV):
-            pieces = [
-                q_buf[k * per_kv + t, beams, h * HD : (h + 1) * HD]
+            spots = [
+                (k * per_kv + t, slice((j * HALF + b) * heads_here, (j * HALF + b + 1) * heads_here))
+                for b in range(HALF)
                 for t in range(per_kv)
-                for h in range(heads_here)
             ]
-            query = jnp.concatenate(pieces, axis=0)
+            query = jnp.concatenate([q_buf[chip, rows, :] for chip, rows in spots], axis=0)
             turned = query * cosine + pltpu.roll(query, HD // 2, 1) * sines
             turned = (turned * HD ** (-0.5)).astype(bf16)
-            keys = [prefix_buf[j, 0, 0, k], prefix_buf[j, 1, 0, k]]
-            values = [prefix_buf[j, 0, 1, k], prefix_buf[j, 1, 1, k]]
-            scores = [lax.dot_general(turned, key, nt, preferred_element_type=f32) for key in keys]
-            for b in range(HALF):
-                r = j * HALF + b
-                raw = lax.dot_general(turned, page_buf[r, 0, k], nt, preferred_element_type=f32)
-                scores.append(jnp.where(masks[b], raw, big_negative))
-                values.append(page_buf[r, 1, k])
-            new_key = spread(new_ref[beams, k * HD : (k + 1) * HD])
-            new_value = spread(new_ref[beams, (KV + k) * HD : (KV + k + 1) * HD])
+            prefix_scores = [
+                lax.dot_general(turned, prefix_buf[j, side, 0, k], nt, preferred_element_type=f32)
+                for side in range(2)
+            ]
+            page_scores = jnp.concatenate(
+                [
+                    jnp.where(
+                        masks[b],
+                        lax.dot_general(
+                            turned[b * beam_rows : (b + 1) * beam_rows],
+                            page_buf[j * HALF + b, 0, k],
+                            nt,
+                            preferred_element_type=f32,
+                        ),
+                        big_negative,
+                    )
+                    for b in range(HALF)
+                ],
+                axis=0,
+            )
+            new_key = spread(new_ref, slice(k * HD, (k + 1) * HD))
+            new_value = spread(new_ref, slice((KV + k) * HD, (KV + k + 1) * HD))
             new_score = jnp.sum(turned.astype(f32) * new_key, axis=1, keepdims=True)
+            scores = prefix_scores + [page_scores]
             highest = new_score
             for score in scores:
                 highest = jnp.maximum(highest, jnp.max(score, axis=1, keepdims=True))
+            weights = [jnp.exp(score - highest) for score in scores]
             new_weight = jnp.exp(new_score - highest)
             weight_sum = new_weight
+            for weight in weights:
+                weight_sum = weight_sum + jnp.sum(weight, axis=1, keepdims=True)
             weighted = new_weight.astype(bf16).astype(f32) * new_value
-            for score, value in zip(scores, values):
-                weight = jnp.exp(score - highest)
-                weight_sum = weight_sum + jnp.sum(weight, axis=1, keepdims=True)
+            for side in range(2):
                 weighted = weighted + jnp.dot(
-                    weight.astype(bf16), value, preferred_element_type=f32
+                    weights[side].astype(bf16),
+                    prefix_buf[j, side, 1, k],
+                    preferred_element_type=f32,
                 )
+            page_weight = weights[2].astype(bf16)
+            weighted = weighted + jnp.concatenate(
+                [
+                    jnp.dot(
+                        page_weight[b * beam_rows : (b + 1) * beam_rows],
+                        page_buf[j * HALF + b, 1, k],
+                        preferred_element_type=f32,
+                    )
+                    for b in range(HALF)
+                ],
+                axis=0,
+            )
             result = weighted / weight_sum
-            for t in range(per_kv):
-                for h in range(heads_here):
-                    at = (t * heads_here + h) * HALF
-                    o_buf[k * per_kv + t, beams, h * HD : (h + 1) * HD] = result[at : at + HALF]
+            for n, (chip, rows) in enumerate(spots):
+                o_buf[chip, rows, :] = result[n * heads_here : (n + 1) * heads_here]
     out_ref[...] = o_buf[...].astype(bf16)
 
 
 def attend(queries, cosine, sines, new_rows, prefix_own, prefix_far, suffix_own, suffix_far,
            source, row, page_len):
-    devices, rows, width = queries.shape
+    rows = suffix_own.shape[0]
     prompts = rows // HALF
     part = prefix_own.shape[4]
     page = suffix_own.shape[3]
@@ -394,21 +473,21 @@
             far_len = send(lengths, to_core)
             prefix_far = send(prefix_kv, to_core)
             wq_send = others_half(w_query, plan, chips, True)
-            a, b, far_len, prefix_far, wq_send = tied(a, b, far_len, prefix_far, wq_send)
+            beside = tables(far_len)
+            a, b, prefix_far, wq_send, *beside = tied(a, b, prefix_far, wq_send, *beside)
+            cosine, sines, new_rows, source, page_row, page_len = beside
             wq_far = send(wq_send, to_core)
         else:
             beside = []
             fresh = blocks[own_done:]
             if s == 2:
                 own_total = query_terms(None, fresh, w_query, None, plan, 0)
-                wo_send = others_half(w_out, plan, chips, False)
-                beside = [wo_send] + list(tables(far_len))
+                w_whole, *own_total = tied(w_out, *own_total)
+                wo_send = others_half(w_whole, plan, chips, False)
+                beside = [wo_send]
             elif s == 3:
                 own_total = query_terms(own_total, fresh, w_query, None, plan, own_done)
                 far_total = list(query_terms(None, blocks, None, wq_far, plan, 0))
-                wo_send, suffix_in, far_total[0] = tied(wo_send, suffix_kv, far_total[0])
-                wo_far = send(wo_send, to_core)
-                suffix_far = send(suffix_in, to_core)
             else:
                 own_total, far_total = query_terms(
                     own_total + far_total, fresh, w_query, wq_far, plan, own_done
@@ -420,35 +499,41 @@
             if s > 2:
                 far_total, beside = beside[:1], beside[1:]
             if s == 2:
-                wo_send, cosine, sines, new_rows, source, page_row, page_len = beside
+                wo_send, suffix_in = tied(*beside, suffix_kv)
+                wo_far = send(wo_send, to_core)
+                suffix_far = send(suffix_in, to_core)
             own_done = len(blocks)
         if s < hops:
             blocks += [[(a, 0)], [(b, 0)]]
         else:
             blocks.append([(a, 0), (b, cut)])
-    own_total, far_total = query_terms(
-        own_total + far_total, blocks[own_done:], w_query, wq_far, plan, own_done
+    keep, give = query_terms(
+        own_total + far_total, blocks[own_done:], w_query, wq_far, plan, own_done, True
     )
-    query = own_total + send(far_total, to_core)
-    query = query.astype(bf16).reshape(count, rows_here, -1)
+    query = (keep + send(give, to_core)).astype(bf16).reshape(chips, -1, HD)
+    same_core = [[2 * chip + side for chip in range(chips)] for side in range(2)]
+
+    def exchange(values):
+        return lax.all_to_all(
+            values, "tensor", split_axis=0, concat_axis=0, axis_index_groups=same_core, tiled=True
+        )
 
     query, suffix_far, wo_far = tied(query, suffix_far, wo_far)
-    queries = lax.all_to_all(query, "tensor", split_axis=0, concat_axis=0, tiled=True)
-    heads = attend(queries, cosine, sines, new_rows, prefix_kv, prefix_far, suffix_kv, suffix_far,
-                   source, page_row, page_len)
-    heads = lax.all_to_all(heads, "tensor", split_axis=0, concat_axis=0, tiled=True)
-    own = heads.reshape(rows_all, -1)
-    far = send(own, to_core)
+    heads = exchange(
+        attend(exchange(query), cosine, sines, new_rows, prefix_kv, prefix_far, suffix_kv,
+               suffix_far, source, page_row, page_len)
+    ).reshape(-1, HD)
+    heads = (heads, send(heads, to_core))
 
     width = w_out.shape[1] // count
 
-    def out(first, amount, kind, parts=1):
-        return out_terms(own, far, w_out, wo_far, plan, chips + first, amount, width, kind, parts)
-
-    up, down = tied(*out(0, 1, bf16, 2))
+    def out(heads, first, amount, kind, parts=1):
+        return out_terms(heads, w_out, wo_far, plan, chips + first, amount, width, kind, parts)
+
+    up, down, heads = tied(*out(heads, 0, 1, bf16, 2))
     a, b = send(up, onward), send(down, backward)
     for s in range(hops - 1, 0, -1):
-        up, down = out(1 + 2 * (hops - 1 - s), 2, f32)
+        up, down = out(heads, 1 + 2 * (hops - 1 - s), 2, f32)
         a, b, up, down = tied(a, b, up, down)
         a, b = a.astype(f32), b.astype(f32)
         if s == hops - 1:
@@ -458,7 +543,7 @@
             up, down = up + a, down + b
         a, b = tied(up.astype(bf16), down.astype(bf16))
         a, b = send(a, onward), send(b, backward)
-    [own_term] = out(chips - 1, 1, f32)
+    [own_term] = out(heads, chips - 1, 1, f32)
     a, b, own_term = tied(a, b, own_term)
     return (own_term + a.astype(f32) + b.astype(f32)).astype(bf16)
 

time: 143 us -> 126 us (0.88)
  waiting for transfers between devices: 38.1 us -> 26.7 us
  blocking collectives: 26.6 us -> 23 us
    ppermute x23, waiting for transfers between devices: 38.1 us -> 26.7 us  [send(): return lax.ppermute(block, 'tensor', route)]
    all_to_all x2, blocking collectives: 26.6 us -> 23 us  [exchange(): lax.all_to_all(values, 'tensor', split_axis=0, concat_axis=0, axis_index_...]
  transfers between devices with their start and end apart: 23 -> 23, of which waited for: 18 -> 17; matrix products, arithmetic and copies ran while one was open for 2% -> 1% of each run, Pallas kernels for 27% -> 34%
where the time goes in v2:
time: 126 us; the launch traced here: 125 us
  Pallas kernels  53.4 us (42%)
  waiting for transfers between devices  26.7 us (21%)
  blocking collectives  23 us (18%)
  starting transfers between devices  18.3 us (15%)
  other arithmetic  1.97 us (2%)
  local copies, waits for them, and re-layouts  1.38 us (1%)
    ppermute x23, waiting for transfers between devices, send(): return lax.ppermute(block, 'tensor', route)  26.7 us
    all_to_all x2, blocking collectives, exchange(): lax.all_to_all(values, 'tensor', split_axis=0, concat_axis=0, axis_index_...  23 us
    ppermute x23, starting transfers between devices, send(): return lax.ppermute(block, 'tensor', route)  18.3 us
    pallas_call x5, Pallas kernels, out_terms(): pl.pallas_call(functools.partial(out_kernel, first, amount, parts, openin...  15.5 us
    pallas_call x5, Pallas kernels, query_terms(): pl.pallas_call(functools.partial(query_kernel, bases, first, far, bool(to...  15.4 us
    pallas_call x2, Pallas kernels, others_half(): pl.pallas_call(functools.partial(split_kernel, chips, by_rows), in_specs=...  14 us
    pallas_call x1, Pallas kernels, attend(): pl.pallas_call(attend_kernel, in_specs=[smem] * 3 + [vmem] * 4 + [anywher...  8.55 us
  transfers between devices with their start and end apart: 23, of which 17 were waited for; matrix products, arithmetic and copies ran while one was open for 1% of the time, Pallas kernels for 34%

profile of v2, /device:TPU:0, one launch (start us, length us, event | category | flops | bytes accessed | tf_op | source)
XLA Modules:
  0.0 125.2 jit_solution(13591480299313484102)
XLA Ops:
  0.5 2.6 %collective-permute-start = (bf16[192,1024]{1,0:T(8,128)(2,1)}, bf16[192,1024]{1,0:T(8,128)(2,1)S(1)}, u32[]{:S(2)}, u32[]{:S(2)}) collective-permute-start(bf16[192,1024]{1,0:T(8,128)(2,1)} %refs_0_.3), channel_id=1, source_target_pairs={{0,4},{1,5},{4,8},{5,9},{8,12},{9,13},{12,14},{13,15},{14,10},{15,... | collective-permute-start | bytes 1179656 | tf_op jit(solution)/shard_map/ppermute | solution.py:32
  4.0 7.0 %shard_map.91 = bf16[8192,512]{1,0:T(8,128)(2,1)} custom-call(s32[17]{0:T(128)S(1)} %dynamic-slice_bitcast_fusion.plan_ref, bf16[16384,512]{1,0:T(8,128)(2,1)} %refs_2_.6), custom_call_target="tpu_custom_call" | custom-call | flops 1000 | bytes 1000 | tf_op jit(solution)/shard_map/pallas_call | solution.py:84
  14.5 1.6 %collective-permute-start.4 = (bf16[192,1024]{1,0:T(8,128)(2,1)S(1)}, bf16[192,1024]{1,0:T(8,128)(2,1)S(1)}, u32[]{:S(2)}, u32[]{:S(2)}) collective-permute-start(bf16[192,1024]{1,0:T(8,128)(2,1)S(1)} %collective-permute-done.refs_1_), channel_id=1, source_target_pairs={{0,4},{1,5},{4,8},{5,9},{8,12},{9,13},{12,14},{13,15},{14,10},{15,... | collective-permute-start | bytes 1179656 | tf_op jit(solution)/shard_map/ppermute | solution.py:32
  16.5 3.1 %shard_map.92.refs_3_ = f32[192,512]{1,0:T(8,128)S(1)} custom-call(s32[17]{0:T(128)S(1)} %dynamic-slice_bitcast_fusion.plan_ref, bf16[192,1024]{1,0:T(8,128)(2,1)S(1)} %copy-done.1, bf16[192,1024]{1,0:T(8,128)(2,1)S(1)} %collective-permute-done.refs_1_, bf16[192,1024]{1,0:T(8,128)(2,1)S(1)} %collective-permute-done.1.refs_2_, bf16[16384,512]{1,0:T(8,128)(2,1)} %refs_2_.6), custom_call_target="tpu_custom_call" | custom-call | flops 1000 | bytes 1000 | tf_op jit(solution)/shard_map/pallas_call | solution.py:172
  19.6 7.1 %shard_map.93 = bf16[512,8192]{1,0:T(8,128)(2,1)} custom-call(s32[17]{0:T(128)S(1)} %dynamic-slice_bitcast_fusion.plan_ref, bf16[512,16384]{1,0:T(8,128)(2,1)} %refs_1_.7), custom_call_target="tpu_custom_call" | custom-call | flops 1000 | bytes 1000 | tf_op jit(solution)/shard_map/pallas_call | solution.py:84
  29.9 2.5 %shard_map.94.refs_4_ = f32[192,512]{1,0:T(8,128)S(1)} custom-call(s32[17]{0:T(128)S(1)} %dynamic-slice_bitcast_fusion.plan_ref, bf16[192,1024]{1,0:T(8,128)(2,1)S(1)} %collective-permute-done.4.refs_0_.refs_3_, bf16[192,1024]{1,0:T(8,128)(2,1)S(1)} %collective-permute-done.5.refs_1_.refs_4_, bf16[16384,512]{1,0:T(8,128)(2,1)} %refs_2_.6, ...), custom_call_target="tpu_custom_call" | custom-call | flops 1000 | bytes 1000 | tf_op jit(solution)/shard_map/pallas_call | solution.py:172
  32.4 3.5 %shard_map.95.refs_5_ = f32[192,512]{1,0:T(8,128)S(1)} custom-call(s32[17]{0:T(128)S(1)} %dynamic-slice_bitcast_fusion.plan_ref, bf16[192,1024]{1,0:T(8,128)(2,1)S(1)} %copy-done.1, bf16[192,1024]{1,0:T(8,128)(2,1)S(1)} %collective-permute-done.refs_1_, bf16[192,1024]{1,0:T(8,128)(2,1)S(1)} %collective-permute-done.1.refs_2_, ...), custom_call_target="tpu_custom_call" | custom-call | flops 1000 | bytes 1000 | tf_op jit(solution)/shard_map/pallas_call | solution.py:172
  35.8 3.1 %collective-permute-done.6.refs_0_ = bf16[192,1024]{1,0:T(8,128)(2,1)S(1)} collective-permute-done((bf16[192,1024]{1,0:T(8,128)(2,1)S(1)}, bf16[192,1024]{1,0:T(8,128)(2,1)S(1)}, u32[]{:S(2)}, u32[]{:S(2)}) %collective-permute-start.6) | collective-permute-done | bytes 393248 | tf_op jit(solution)/shard_map/ppermute | solution.py:32
  40.8 1.6 %collective-permute-start.9 = (bf16[96,1024]{1,0:T(8,128)(2,1)S(1)}, bf16[96,1024]{1,0:T(8,128)(2,1)S(1)}, u32[]{:S(2)}, u32[]{:S(2)}) collective-permute-start(bf16[96,1024]{1,0:T(8,128)(2,1)S(1)} %slice.20), channel_id=1, source_target_pairs={{0,4},{1,5},{4,8},{5,9},{8,12},{9,13},{12,14},{13,15},{14,10},{15,... | collective-permute-start | bytes 589832 | tf_op jit(solution)/shard_map/ppermute | solution.py:32
  42.4 3.2 %shard_map.96 = (f32[192,512]{1,0:T(8,128)S(1)}, f32[192,512]{1,0:T(8,128)S(1)}) custom-call(s32[17]{0:T(128)S(1)} %dynamic-slice_bitcast_fusion.plan_ref, bf16[192,1024]{1,0:T(8,128)(2,1)S(1)} %collective-permute-done.6.refs_0_, bf16[192,1024]{1,0:T(8,128)(2,1)S(1)} %collective-permute-done.7.refs_1_, bf16[16384,512]{1,0:T(8,128)(2,1)} %refs_2_.6, ...), custom_call_target="tpu_custom_call" | custom-call | flops 1000 | bytes 1000 | tf_op jit(solution)/shard_map/pallas_call | solution.py:172
  46.5 3.2 %shard_map.97 = (f32[768,128]{1,0:T(8,128)S(1)}, f32[768,128]{1,0:T(8,128)S(1)}) custom-call(s32[17]{0:T(128)S(1)} %dynamic-slice_bitcast_fusion.plan_ref, bf16[96,1024]{1,0:T(8,128)(2,1)S(1)} %collective-permute-done.9.refs_0_, bf16[96,1024]{1,0:T(8,128)(2,1)S(1)} %collective-permute-done.10.refs_1_, bf16[16384,512]{1,0:T(8,128)(2,1)} %refs_2_.6, ...), custom_call_target="tpu_custom_call" | custom-call | flops 1000 | bytes 1000 | tf_op jit(solution)/shard_map/pallas_call | solution.py:172
  49.7 1.7 %collective-permute-done.11 = f32[768,128]{1,0:T(8,128)S(1)} collective-permute-done((f32[768,128]{1,0:T(8,128)S(1)}, f32[768,128]{1,0:T(8,128)S(1)}, u32[]{:S(2)}, u32[]{:S(2)}) %collective-permute-start.11) | collective-permute-done | bytes 393248 | tf_op jit(solution)/shard_map/ppermute | solution.py:32
  51.5 12.3 %all_to_all.10.q_ref = bf16[8,96,128]{2,1,0:T(8,128)(2,1)S(1)} all-to-all(bf16[8,96,128]{2,1,0:T(8,128)(2,1)S(1)} %bitcast.8), channel_id=1, replica_groups={{0,2,4,6,8,10,12,14},{1,3,5,7,9,11,13,15},{16,18,20,22,24,26,28,30},{17..., dimensions={0} | all-to-all | bytes 393216 | tf_op jit(solution)/shard_map/all_to_all | solution.py:517
  63.9 8.6 %shard_map.98 = bf16[8,96,128]{2,1,0:T(8,128)(2,1)S(1)} custom-call(s32[12]{0:T(128)S(1)} %get-tuple-element.68.source_ref, s32[12]{0:T(128)S(1)} %fusion.2.row_ref, s32[12]{0:T(128)S(1)} %get-tuple-element.70.length_ref, bf16[8,96,128]{2,1,0:T(8,128)(2,1)S(1)} %all_to_all.10.q_ref, f32[12,128]{1,0:T(8,128)S(1)} %get-tuple-element.95.cos_ref, ...), custom_call_target="tpu_custom_call" | custom-call | flops 503316480 | bytes 12582912 | tf_op jit(solution)/shard_map/pallas_call | solution.py:402
  72.4 10.7 %all_to_all.11 = bf16[8,96,128]{2,1,0:T(8,128)(2,1)S(1)} all-to-all(bf16[8,96,128]{2,1,0:T(8,128)(2,1)S(1)} %shard_map.98), channel_id=1, replica_groups={{0,2,4,6,8,10,12,14},{1,3,5,7,9,11,13,15},{16,18,20,22,24,26,28,30},{17..., dimensions={0} | all-to-all | bytes 393216 | tf_op jit(solution)/shard_map/all_to_all | solution.py:517
  84.6 2.7 %shard_map.99 = (bf16[96,1024]{1,0:T(8,128)(2,1)S(1)}, bf16[96,1024]{1,0:T(8,128)(2,1)S(1)}, bf16[192,1024]{1,0:T(8,128)(2,1)S(1)}) custom-call(s32[17]{0:T(128)S(1)} %dynamic-slice_bitcast_fusion.plan_ref, bf16[768,128]{1,0:T(8,128)(2,1)S(1)} %bitcast.5, bf16[768,128]{1,0:T(8,128)(2,1)S(1)} %collective-permute-done.14.refs_1_, bf16[512,16384]{1,0:T(8,128)(2,1)} %refs_1_.7, ...), custom_call_target="tpu_custom_call" | custom-call | flops 1000 | bytes 1000 | tf_op jit(solution)/shard_map/pallas_call | solution.py:252
  87.6 1.8 %collective-permute-start.16 = (bf16[96,1024]{1,0:T(8,128)(2,1)S(1)}, bf16[96,1024]{1,0:T(8,128)(2,1)S(1)}, u32[]{:S(2)}, u32[]{:S(2)}) collective-permute-start(bf16[96,1024]{1,0:T(8,128)(2,1)S(1)} %get-tuple-element.102), channel_id=1, source_target_pairs={{0,2},{1,3},{4,0},{5,1},{8,4},{9,5},{12,8},{13,9},{14,12},{15,13},... | collective-permute-start | bytes 589832 | tf_op jit(solution)/shard_map/ppermute | solution.py:32
  89.4 3.4 %shard_map.100 = (f32[192,1024]{1,0:T(8,128)S(1)}, f32[192,1024]{1,0:T(8,128)S(1)}) custom-call(s32[17]{0:T(128)S(1)} %dynamic-slice_bitcast_fusion.plan_ref, bf16[192,1024]{1,0:T(8,128)(2,1)S(1)} %get-tuple-element.103.refs_0_, bf16[512,16384]{1,0:T(8,128)(2,1)} %refs_1_.7, bf16[512,8192]{1,0:T(8,128)(2,1)} %collective-permute-done.13.refs_3_.refs_2_), custom_call_target="tpu_custom_call" | custom-call | flops 1000 | bytes 1000 | tf_op jit(solution)/shard_map/pallas_call | solution.py:252
  96.6 3.4 %shard_map.101 = (f32[192,1024]{1,0:T(8,128)S(1)}, f32[192,1024]{1,0:T(8,128)S(1)}) custom-call(s32[17]{0:T(128)S(1)} %dynamic-slice_bitcast_fusion.plan_ref, bf16[192,1024]{1,0:T(8,128)(2,1)S(1)} %get-tuple-element.103.refs_0_, bf16[512,16384]{1,0:T(8,128)(2,1)} %refs_1_.7, bf16[512,8192]{1,0:T(8,128)(2,1)} %collective-permute-done.13.refs_3_.refs_2_), custom_call_target="tpu_custom_call" | custom-call | flops 1000 | bytes 1000 | tf_op jit(solution)/shard_map/pallas_call | solution.py:252
  100.0 4.9 %collective-permute-done.17 = bf16[192,1024]{1,0:T(8,128)(2,1)S(1)} collective-permute-done((bf16[192,1024]{1,0:T(8,128)(2,1)S(1)}, bf16[192,1024]{1,0:T(8,128)(2,1)S(1)}, u32[]{:S(2)}, u32[]{:S(2)}) %collective-permute-start.17) | collective-permute-done | bytes 393248 | tf_op jit(solution)/shard_map/ppermute | solution.py:32
  107.5 3.4 %shard_map.102 = (f32[192,1024]{1,0:T(8,128)S(1)}, f32[192,1024]{1,0:T(8,128)S(1)}) custom-call(s32[17]{0:T(128)S(1)} %dynamic-slice_bitcast_fusion.plan_ref, bf16[192,1024]{1,0:T(8,128)(2,1)S(1)} %get-tuple-element.103.refs_0_, bf16[512,16384]{1,0:T(8,128)(2,1)} %refs_1_.7, bf16[512,8192]{1,0:T(8,128)(2,1)} %collective-permute-done.13.refs_3_.refs_2_), custom_call_target="tpu_custom_call" | custom-call | flops 1000 | bytes 1000 | tf_op jit(solution)/shard_map/pallas_call | solution.py:252
  110.8 3.7 %collective-permute-done.19 = bf16[192,1024]{1,0:T(8,128)(2,1)S(1)} collective-permute-done((bf16[192,1024]{1,0:T(8,128)(2,1)S(1)}, bf16[192,1024]{1,0:T(8,128)(2,1)S(1)}, u32[]{:S(2)}, u32[]{:S(2)}) %collective-permute-start.19) | collective-permute-done | bytes 393248 | tf_op jit(solution)/shard_map/ppermute | solution.py:32
  117.0 2.7 %shard_map.103 = f32[192,1024]{1,0:T(8,128)S(1)} custom-call(s32[17]{0:T(128)S(1)} %dynamic-slice_bitcast_fusion.plan_ref, bf16[192,1024]{1,0:T(8,128)(2,1)S(1)} %get-tuple-element.103.refs_0_, bf16[512,16384]{1,0:T(8,128)(2,1)} %refs_1_.7, bf16[512,8192]{1,0:T(8,128)(2,1)} %collective-permute-done.13.refs_3_.refs_2_), custom_call_target="tpu_custom_call" | custom-call | flops 1000 | bytes 1000 | tf_op jit(solution)/shard_map/pallas_call | solution.py:252
  119.8 3.1 %collective-permute-done.21 = bf16[192,1024]{1,0:T(8,128)(2,1)S(1)} collective-permute-done((bf16[192,1024]{1,0:T(8,128)(2,1)S(1)}, bf16[192,1024]{1,0:T(8,128)(2,1)S(1)}, u32[]{:S(2)}, u32[]{:S(2)}) %collective-permute-start.21) | collective-permute-done | bytes 393248 | tf_op jit(solution)/shard_map/ppermute | solution.py:32
  (84 shorter events, 24.3 us)
Async XLA Ops:
  0.0 14.5 %collective-permute-start.2 = (bf16[1,3,2,4,512,128]{5,4,3,2,1,0:T(8,128)(2,1)}, bf16[1,3,2,4,512,128]{5,4,3,2,1,0:T(8,128)(2,1)}, u32[]{:S(2)}, u32[]{:S(2)}) collective-permute-start(bf16[1,3,2,4,512,128]{5,4,3,2,1,0:T(8,128)(2,1)} %prefix_own.1), channel_id=1, source_target_pairs={{0,1},{1,0},{2,3},{3,2},{4,5},{5,4},{6,7},{7,6},{8,9},{9,8},{10,11... | collective-permute-start | bytes 9437192 | tf_op jit(solution)/shard_map/ppermute | solution.py:32
  0.5 12.5 %collective-permute-start = (bf16[192,1024]{1,0:T(8,128)(2,1)}, bf16[192,1024]{1,0:T(8,128)(2,1)S(1)}, u32[]{:S(2)}, u32[]{:S(2)}) collective-permute-start(bf16[192,1024]{1,0:T(8,128)(2,1)} %refs_0_.3), channel_id=1, source_target_pairs={{0,4},{1,5},{4,8},{5,9},{8,12},{9,13},{12,14},{13,15},{14,10},{15,... | collective-permute-start | bytes 1179656 | tf_op jit(solution)/shard_map/ppermute | solution.py:32
  3.0 11.5 %collective-permute-start.1 = (bf16[192,1024]{1,0:T(8,128)(2,1)}, bf16[192,1024]{1,0:T(8,128)(2,1)S(1)}, u32[]{:S(2)}, u32[]{:S(2)}) collective-permute-start(bf16[192,1024]{1,0:T(8,128)(2,1)} %refs_0_.3), channel_id=1, source_target_pairs={{0,2},{1,3},{4,0},{5,1},{8,4},{9,5},{12,8},{13,9},{14,12},{15,13},... | collective-permute-start | bytes 1179656 | tf_op jit(solution)/shard_map/ppermute | solution.py:32
  3.0 8.4 %collective-permute-start.3 = (s32[12]{0:T(128)}, s32[12]{0:T(128)S(1)}, u32[]{:S(2)}, u32[]{:S(2)}) collective-permute-start(s32[12]{0:T(128)} %param.16), channel_id=1, source_target_pairs={{0,1},{1,0},{2,3},{3,2},{4,5},{5,4},{6,7},{7,6},{8,9},{9,8},{10,11... | collective-permute-start | bytes 152 | tf_op jit(solution)/shard_map/ppermute | solution.py:32
  14.5 17.9 %collective-permute-start.8 = (bf16[8192,512]{1,0:T(8,128)(2,1)}, bf16[8192,512]{1,0:T(8,128)(2,1)}, u32[]{:S(2)}, u32[]{:S(2)}) collective-permute-start(bf16[8192,512]{1,0:T(8,128)(2,1)} %shard_map.91), channel_id=1, source_target_pairs={{0,1},{1,0},{2,3},{3,2},{4,5},{5,4},{6,7},{7,6},{8,9},{9,8},{10,11... | collective-permute-start | bytes 25165832 | tf_op jit(solution)/shard_map/ppermute | solution.py:32
  14.5 12.2 %collective-permute-start.4 = (bf16[192,1024]{1,0:T(8,128)(2,1)S(1)}, bf16[192,1024]{1,0:T(8,128)(2,1)S(1)}, u32[]{:S(2)}, u32[]{:S(2)}) collective-permute-start(bf16[192,1024]{1,0:T(8,128)(2,1)S(1)} %collective-permute-done.refs_1_), channel_id=1, source_target_pairs={{0,4},{1,5},{4,8},{5,9},{8,12},{9,13},{12,14},{13,15},{14,10},{15,... | collective-permute-start | bytes 1179656 | tf_op jit(solution)/shard_map/ppermute | solution.py:32
  16.1 11.2 %collective-permute-start.5 = (bf16[192,1024]{1,0:T(8,128)(2,1)S(1)}, bf16[192,1024]{1,0:T(8,128)(2,1)S(1)}, u32[]{:S(2)}, u32[]{:S(2)}) collective-permute-start(bf16[192,1024]{1,0:T(8,128)(2,1)S(1)} %collective-permute-done.1.refs_2_), channel_id=1, source_target_pairs={{0,2},{1,3},{4,0},{5,1},{8,4},{9,5},{12,8},{13,9},{14,12},{15,13},... | collective-permute-start | bytes 1179656 | tf_op jit(solution)/shard_map/ppermute | solution.py:32
  27.3 24.2 %collective-permute-start.13 = (bf16[512,8192]{1,0:T(8,128)(2,1)}, bf16[512,8192]{1,0:T(8,128)(2,1)}, u32[]{:S(2)}, u32[]{:S(2)}) collective-permute-start(bf16[512,8192]{1,0:T(8,128)(2,1)} %shard_map.93), channel_id=1, source_target_pairs={{0,1},{1,0},{2,3},{3,2},{4,5},{5,4},{6,7},{7,6},{8,9},{9,8},{10,11... | collective-permute-start | bytes 25165832 | tf_op jit(solution)/shard_map/ppermute | solution.py:32
  27.3 24.2 %collective-permute-start.12 = (bf16[12,2,4,256,128]{4,3,2,1,0:T(8,128)(2,1)S(1)}, bf16[12,2,4,256,128]{4,3,2,1,0:T(8,128)(2,1)}, u32[]{:S(2)}, u32[]{:S(2)}) collective-permute-start(bf16[12,2,4,256,128]{4,3,2,1,0:T(8,128)(2,1)S(1)} %bitcast.7), channel_id=1, source_target_pairs={{0,1},{1,0},{2,3},{3,2},{4,5},{5,4},{6,7},{7,6},{8,9},{9,8},{10,11... | collective-permute-start | bytes 18874376 | tf_op jit(solution)/shard_map/ppermute | solution.py:32
  27.8 11.1 %collective-permute-start.6 = (bf16[192,1024]{1,0:T(8,128)(2,1)S(1)}, bf16[192,1024]{1,0:T(8,128)(2,1)S(1)}, u32[]{:S(2)}, u32[]{:S(2)}) collective-permute-start(bf16[192,1024]{1,0:T(8,128)(2,1)S(1)} %collective-permute-done.4.refs_0_.refs_3_), channel_id=1, source_target_pairs={{0,4},{1,5},{4,8},{5,9},{8,12},{9,13},{12,14},{13,15},{14,10},{15,... | collective-permute-start | bytes 1179656 | tf_op jit(solution)/shard_map/ppermute | solution.py:32
  29.4 10.8 %collective-permute-start.7 = (bf16[192,1024]{1,0:T(8,128)(2,1)S(1)}, bf16[192,1024]{1,0:T(8,128)(2,1)S(1)}, u32[]{:S(2)}, u32[]{:S(2)}) collective-permute-start(bf16[192,1024]{1,0:T(8,128)(2,1)S(1)} %collective-permute-done.5.refs_1_.refs_4_), channel_id=1, source_target_pairs={{0,2},{1,3},{4,0},{5,1},{8,4},{9,5},{12,8},{13,9},{14,12},{15,13},... | collective-permute-start | bytes 1179656 | tf_op jit(solution)/shard_map/ppermute | solution.py:32
  40.2 5.8 %collective-permute-start.10 = (bf16[96,1024]{1,0:T(8,128)(2,1)S(1)}, bf16[96,1024]{1,0:T(8,128)(2,1)S(1)}, u32[]{:S(2)}, u32[]{:S(2)}) collective-permute-start(bf16[96,1024]{1,0:T(8,128)(2,1)S(1)} %slice.21), channel_id=1, source_target_pairs={{0,2},{1,3},{4,0},{5,1},{8,4},{9,5},{12,8},{13,9},{14,12},{15,13},... | collective-permute-start | bytes 589832 | tf_op jit(solution)/shard_map/ppermute | solution.py:32
  40.8 5.7 %collective-permute-start.9 = (bf16[96,1024]{1,0:T(8,128)(2,1)S(1)}, bf16[96,1024]{1,0:T(8,128)(2,1)S(1)}, u32[]{:S(2)}, u32[]{:S(2)}) collective-permute-start(bf16[96,1024]{1,0:T(8,128)(2,1)S(1)} %slice.20), channel_id=1, source_target_pairs={{0,4},{1,5},{4,8},{5,9},{8,12},{9,13},{12,14},{13,15},{14,10},{15,... | collective-permute-start | bytes 589832 | tf_op jit(solution)/shard_map/ppermute | solution.py:32
  46.5 17.4 %copy-start = (bf16[1,3,2,4,512,128]{5,4,3,2,1,0:T(8,128)(2,1)S(1)}, bf16[1,3,2,4,512,128]{5,4,3,2,1,0:T(8,128)(2,1)}, u32[]{:S(2)}) copy-start(bf16[1,3,2,4,512,128]{5,4,3,2,1,0:T(8,128)(2,1)} %prefix_own.1) | copy-start | bytes 9437188
  49.7 1.8 %collective-permute-start.11 = (f32[768,128]{1,0:T(8,128)S(1)}, f32[768,128]{1,0:T(8,128)S(1)}, u32[]{:S(2)}, u32[]{:S(2)}) collective-permute-start(f32[768,128]{1,0:T(8,128)S(1)} %get-tuple-element.90), channel_id=1, source_target_pairs={{0,1},{1,0},{2,3},{3,2},{4,5},{5,4},{6,7},{7,6},{8,9},{9,8},{10,11... | collective-permute-start | bytes 1179656 | tf_op jit(solution)/shard_map/ppermute | solution.py:32
  83.1 1.4 %collective-permute-start.14 = (bf16[768,128]{1,0:T(8,128)(2,1)S(1)}, bf16[768,128]{1,0:T(8,128)(2,1)S(1)}, u32[]{:S(2)}, u32[]{:S(2)}) collective-permute-start(bf16[768,128]{1,0:T(8,128)(2,1)S(1)} %bitcast.4), channel_id=1, source_target_pairs={{0,1},{1,0},{2,3},{3,2},{4,5},{5,4},{6,7},{7,6},{8,9},{9,8},{10,11... | collective-permute-start | bytes 589832 | tf_op jit(solution)/shard_map/ppermute | solution.py:32
  87.3 7.0 %collective-permute-start.15 = (bf16[96,1024]{1,0:T(8,128)(2,1)S(1)}, bf16[96,1024]{1,0:T(8,128)(2,1)S(1)}, u32[]{:S(2)}, u32[]{:S(2)}) collective-permute-start(bf16[96,1024]{1,0:T(8,128)(2,1)S(1)} %get-tuple-element.101), channel_id=1, source_target_pairs={{0,4},{1,5},{4,8},{5,9},{8,12},{9,13},{12,14},{13,15},{14,10},{15,... | collective-permute-start | bytes 589832 | tf_op jit(solution)/shard_map/ppermute | solution.py:32
  87.6 6.8 %collective-permute-start.16 = (bf16[96,1024]{1,0:T(8,128)(2,1)S(1)}, bf16[96,1024]{1,0:T(8,128)(2,1)S(1)}, u32[]{:S(2)}, u32[]{:S(2)}) collective-permute-start(bf16[96,1024]{1,0:T(8,128)(2,1)S(1)} %get-tuple-element.102), channel_id=1, source_target_pairs={{0,2},{1,3},{4,0},{5,1},{8,4},{9,5},{12,8},{13,9},{14,12},{15,13},... | collective-permute-start | bytes 589832 | tf_op jit(solution)/shard_map/ppermute | solution.py:32
  94.6 10.3 %collective-permute-start.17 = (bf16[192,1024]{1,0:T(8,128)(2,1)S(1)}, bf16[192,1024]{1,0:T(8,128)(2,1)S(1)}, u32[]{:S(2)}, u32[]{:S(2)}) collective-permute-start(bf16[192,1024]{1,0:T(8,128)(2,1)S(1)} %pad_maximum_fusion), channel_id=1, source_target_pairs={{0,4},{1,5},{4,8},{5,9},{8,12},{9,13},{12,14},{13,15},{14,10},{15,... | collective-permute-start | bytes 1179656 | tf_op jit(solution)/shard_map/ppermute | solution.py:32
  95.5 9.7 %collective-permute-start.18 = (bf16[192,1024]{1,0:T(8,128)(2,1)S(1)}, bf16[192,1024]{1,0:T(8,128)(2,1)S(1)}, u32[]{:S(2)}, u32[]{:S(2)}) collective-permute-start(bf16[192,1024]{1,0:T(8,128)(2,1)S(1)} %pad_maximum_fusion.1), channel_id=1, source_target_pairs={{0,2},{1,3},{4,0},{5,1},{8,4},{9,5},{12,8},{13,9},{14,12},{15,13},... | collective-permute-start | bytes 1179656 | tf_op jit(solution)/shard_map/ppermute | solution.py:32
  105.4 9.1 %collective-permute-start.19 = (bf16[192,1024]{1,0:T(8,128)(2,1)S(1)}, bf16[192,1024]{1,0:T(8,128)(2,1)S(1)}, u32[]{:S(2)}, u32[]{:S(2)}) collective-permute-start(bf16[192,1024]{1,0:T(8,128)(2,1)S(1)} %add_convert_fusion.4), channel_id=1, source_target_pairs={{0,4},{1,5},{4,8},{5,9},{8,12},{9,13},{12,14},{13,15},{14,10},{15,... | collective-permute-start | bytes 1179656 | tf_op jit(solution)/shard_map/ppermute | solution.py:32
  106.3 8.5 %collective-permute-start.20 = (bf16[192,1024]{1,0:T(8,128)(2,1)S(1)}, bf16[192,1024]{1,0:T(8,128)(2,1)S(1)}, u32[]{:S(2)}, u32[]{:S(2)}) collective-permute-start(bf16[192,1024]{1,0:T(8,128)(2,1)S(1)} %add_convert_fusion.3), channel_id=1, source_target_pairs={{0,2},{1,3},{4,0},{5,1},{8,4},{9,5},{12,8},{13,9},{14,12},{15,13},... | collective-permute-start | bytes 1179656 | tf_op jit(solution)/shard_map/ppermute | solution.py:32
  115.0 7.9 %collective-permute-start.21 = (bf16[192,1024]{1,0:T(8,128)(2,1)S(1)}, bf16[192,1024]{1,0:T(8,128)(2,1)S(1)}, u32[]{:S(2)}, u32[]{:S(2)}) collective-permute-start(bf16[192,1024]{1,0:T(8,128)(2,1)S(1)} %add_convert_fusion.2), channel_id=1, source_target_pairs={{0,4},{1,5},{4,8},{5,9},{8,12},{9,13},{12,14},{13,15},{14,10},{15,... | collective-permute-start | bytes 1179656 | tf_op jit(solution)/shard_map/ppermute | solution.py:32
  116.5 7.8 %collective-permute-start.22 = (bf16[192,1024]{1,0:T(8,128)(2,1)S(1)}, bf16[192,1024]{1,0:T(8,128)(2,1)S(1)}, u32[]{:S(2)}, u32[]{:S(2)}) collective-permute-start(bf16[192,1024]{1,0:T(8,128)(2,1)S(1)} %add_convert_fusion.1), channel_id=1, source_target_pairs={{0,2},{1,3},{4,0},{5,1},{8,4},{9,5},{12,8},{13,9},{14,12},{15,13},... | collective-permute-start | bytes 1179656 | tf_op jit(solution)/shard_map/ppermute | solution.py:32
  (6 other events, 52.4 us)

commit v3 on v2

--- a/solution.py
+++ b/solution.py
@@ -96,27 +96,44 @@
     )(plan, whole)
 
 
-def query_kernel(bases, first, far, with_total, closing, plan_ref, *refs):
+def query_kernel(bases, first, far, with_total, fetching, closing, plan_ref, *refs):
     sides = len(far)
+    if fetching:
+        *refs, next_sems = refs
+        *refs, next_weights, buf, sems = refs
+        refs = refs + [buf, sems]
     count = sum(len(group) for group in bases)
     blocks = refs[:count]
-    weights = refs[count : count + sides]
-    before = refs[count + sides : count + 2 * sides] if with_total else None
+    operands = 1 if closing else sides
+    weights = refs[count : count + operands]
+    before = refs[count + operands : count + operands + sides] if with_total else None
     if closing:
-        keep, give, buf, sems, *totals = refs[-4 - sides :]
+        keep, give, *totals = refs[-2 - sides :]
+        buf = weights[0]
     else:
         totals, buf, sems = refs[-sides - 2 : -2], refs[-2], refs[-1]
     depth = buf.shape[1]
     core = plan_ref[plan_ref.shape[0] - 1]
     copies = []
-    for i in range(len(bases)):
+    for i in range(0 if closing else len(bases)):
         for side in range(sides):
             block = plan_ref[first + i]
             block = block if far[side] else 2 * block + core
             rows = pl.ds(pl.multiple_of(block * depth, depth), depth)
             n = i * sides + side
             copies.append(pltpu.make_async_copy(weights[side].at[rows], buf.at[n], sems.at[n]))
-    for copy in copies:
+    later = []
+    if fetching:
+        for side in range(sides):
+            block = plan_ref[first + len(bases)]
+            block = block if far[side] else 2 * block + core
+            rows = pl.ds(pl.multiple_of(block * depth, depth), depth)
+            later.append(
+                pltpu.make_async_copy(
+                    weights[side].at[rows], next_weights.at[side], next_sems.at[side]
+                )
+            )
+    for copy in copies + later:
         copy.start()
     for side in range(sides):
         if with_total:
@@ -127,13 +144,16 @@
     for i, group in enumerate(bases):
         for side in range(sides):
             n = i * sides + side
-            copies[n].wait()
+            if not closing:
+                copies[n].wait()
             for g, base in enumerate(group):
                 rows = pl.ds(base, blocks[at + g].shape[0])
                 totals[side][rows, :] += jnp.dot(
                     blocks[at + g][...], buf[n], preferred_element_type=f32
                 )
         at += len(group)
+    for copy in later:
+        copy.wait()
     if not closing:
         return
     chips = (plan_ref.shape[0] - 1) // 2
@@ -157,7 +177,8 @@
         pl.when(core == side)(functools.partial(hand_out, side))
 
 
-def query_terms(totals, groups, w_own, w_far, plan, first, closing=False):
+def query_terms(totals, groups, w_own, w_far, plan, first, fetched=None, fetching=False):
+    closing = fetched is not None
     blocks = [block for group in groups for block, _ in group]
     bases = [[base for _, base in group] for group in groups]
     depth = blocks[0].shape[1]
@@ -169,95 +190,140 @@
     totals = list(totals) if totals is not None else []
     vmem = pl.BlockSpec(memory_space=pltpu.VMEM)
     shape = (rows * width // HD, HD) if closing else (rows, width)
+    if closing:
+        weights = [fetched]
+        scratch = [pltpu.VMEM((rows, width), f32)] * sides
+    else:
+        scratch = [
+            pltpu.VMEM((sides * len(groups), depth, width), bf16),
+            pltpu.SemaphoreType.DMA((sides * len(groups),)),
+        ] + [pltpu.SemaphoreType.DMA((sides,))] * fetching
     return pl.pallas_call(
-        functools.partial(query_kernel, bases, first, far, bool(totals), closing),
+        functools.partial(query_kernel, bases, first, far, bool(totals), fetching, closing),
         in_specs=[pl.BlockSpec(memory_space=pltpu.SMEM)]
         + [vmem] * len(blocks)
-        + [pl.BlockSpec(memory_space=pl.ANY)] * sides
+        + ([vmem] if closing else [pl.BlockSpec(memory_space=pl.ANY)] * sides)
         + [vmem] * len(totals),
-        out_specs=[vmem] * sides,
-        out_shape=[jax.ShapeDtypeStruct(shape, f32)] * sides,
-        scratch_shapes=[
-            pltpu.VMEM((sides * len(groups), depth, width), bf16),
-            pltpu.SemaphoreType.DMA((sides * len(groups),)),
-        ]
-        + [pltpu.VMEM((rows, width), f32)] * (sides if closing else 0),
+        out_specs=[vmem] * (sides + fetching),
+        out_shape=[jax.ShapeDtypeStruct(shape, f32)] * sides
+        + [jax.ShapeDtypeStruct((sides, depth, width), bf16)] * fetching,
+        scratch_shapes=scratch,
         cost_estimate=BESIDE,
         compiler_params=pltpu.CompilerParams(vmem_limit_bytes=VMEM_LIMIT),
     )(plan, *blocks, *weights, *totals)
 
 
-def out_kernel(first, amount, parts, opening, plan_ref, *refs):
+def column_copies(plan_ref, position, width, w_own, w_far, target, sems):
     core = plan_ref[plan_ref.shape[0] - 1]
-    if opening:
-        mine, other, w_own, w_far = refs[:4]
-        outs, lhs, (buf, sems, mixed, flat) = refs[4:-5], refs[-5], refs[-4:]
-    else:
-        lhs, w_own, w_far = refs[:3]
-        outs, (buf, sems) = refs[3:-2], refs[-2:]
-    width = buf.shape[3]
+    chip = plan_ref[position]
     copies = []
-    for i in range(amount):
-        block = plan_ref[first + i]
-        for side, weights in enumerate((w_own, w_far)):
-            column = block if side else 2 * block + core
-            columns = pl.ds(pl.multiple_of(column * width, width), width)
-            owner = 1 - core if side else core
-            copies.append(
-                pltpu.make_async_copy(weights.at[:, columns], buf.at[i, owner], sems.at[2 * i + side])
-            )
+    for side, (weights, column, owner) in enumerate(
+        ((w_own, 2 * chip + core, core), (w_far, chip, 1 - core))
+    ):
+        columns = pl.ds(pl.multiple_of(column * width, width), width)
+        copies.append(
+            pltpu.make_async_copy(weights.at[:, columns], target.at[owner], sems.at[side])
+        )
+    return copies
+
+
+def column_kernel(first, plan_ref, w_own, w_far, target, sems):
+    copies = column_copies(plan_ref, first, target.shape[2], w_own, w_far, target, sems)
     for copy in copies:
         copy.start()
-    if opening:
-        chips = (plan_ref.shape[0] - 1) // 2
-        rows_here = lhs.shape[0] // (2 * chips)
-        heads = lhs.shape[1] // HD
-        halves = [mine[...].astype(f32), other[...].astype(f32)]
-        for side in range(2):
-            mixed[...] = jnp.where(core == side, halves[0], halves[1])
-            for h in range(heads):
-                columns = slice(h * HD, (h + 1) * HD)
-                for chip in range(chips):
-                    rows = slice((2 * chip + side) * rows_here, (2 * chip + side + 1) * rows_here)
-                    start = chip * rows_here * heads + h
-                    flat[rows, columns] = mixed[pl.ds(start, rows_here, heads), :]
-        lhs[...] = flat[...].astype(bf16)
+    for copy in copies:
+        copy.wait()
+
+
+def first_columns(w_own, w_far, plan, first, width):
+    anywhere = pl.BlockSpec(memory_space=pl.ANY)
+    return pl.pallas_call(
+        functools.partial(column_kernel, first),
+        in_specs=[pl.BlockSpec(memory_space=pltpu.SMEM)] + [anywhere] * 2,
+        out_specs=pl.BlockSpec(memory_space=pltpu.VMEM),
+        out_shape=jax.ShapeDtypeStruct((2, w_own.shape[0], width), bf16),
+        scratch_shapes=[pltpu.SemaphoreType.DMA((2,))],
+        cost_estimate=BESIDE,
+        compiler_params=pltpu.CompilerParams(vmem_limit_bytes=VMEM_LIMIT),
+    )(plan, w_own, w_far)
+
+
+def opening_kernel(parts, plan_ref, mine, other, columns_ref, *refs):
+    outs, lhs, mixed, flat = refs[:-3], refs[-3], refs[-2], refs[-1]
+    core = plan_ref[plan_ref.shape[0] - 1]
+    chips = (plan_ref.shape[0] - 1) // 2
+    rows_here = lhs.shape[0] // (2 * chips)
+    heads = lhs.shape[1] // HD
+    halves = [mine[...].astype(f32), other[...].astype(f32)]
+    for side in range(2):
+        mixed[side] = jnp.where(core == side, halves[0], halves[1])
+        for h in range(heads):
+            for chip in range(chips):
+                rows = slice((2 * chip + side) * rows_here, (2 * chip + side + 1) * rows_here)
+                start = chip * rows_here * heads + h
+                flat[rows, h * HD : (h + 1) * HD] = mixed[side, pl.ds(start, rows_here, heads), :]
+    lhs[...] = flat[...].astype(bf16)
+    depth = columns_ref.shape[1]
+    value = jnp.dot(lhs[:, :depth], columns_ref[0], preferred_element_type=f32)
+    value = value + jnp.dot(lhs[:, depth:], columns_ref[1], preferred_element_type=f32)
+    rows = value.shape[0] // parts
+    for p in range(parts):
+        outs[p][...] = value[p * rows : (p + 1) * rows].astype(bf16)
+
+
+def opening_terms(mine, other, columns, plan, parts):
+    depth, width = columns.shape[1:]
+    rows = mine.size // depth
+    vmem = pl.BlockSpec(memory_space=pltpu.VMEM)
+    return pl.pallas_call(
+        functools.partial(opening_kernel, parts),
+        in_specs=[pl.BlockSpec(memory_space=pltpu.SMEM)] + [vmem] * 3,
+        out_specs=[vmem] * (parts + 1),
+        out_shape=[jax.ShapeDtypeStruct((rows // parts, width), bf16)] * parts
+        + [jax.ShapeDtypeStruct((rows, 2 * depth), bf16)],
+        scratch_shapes=[
+            pltpu.VMEM((2,) + mine.shape, f32),
+            pltpu.VMEM((rows, 2 * depth), f32),
+        ],
+        cost_estimate=BESIDE,
+        compiler_params=pltpu.CompilerParams(vmem_limit_bytes=VMEM_LIMIT),
+    )(plan, mine, other, columns)
+
+
+def out_kernel(first, amount, plan_ref, lhs, w_own, w_far, *refs):
+    outs, buf, sems = refs[:-2], refs[-2], refs[-1]
+    depth, width = buf.shape[2:]
+    copies = [
+        column_copies(plan_ref, first + i, width, w_own, w_far, buf.at[i], sems.at[i])
+        for i in range(amount)
+    ]
+    for pair in copies:
+        for copy in pair:
+            copy.start()
     for i in range(amount):
-        copies[2 * i].wait()
-        copies[2 * i + 1].wait()
-        depth = buf.shape[2]
+        for copy in copies[i]:
+            copy.wait()
         value = jnp.dot(lhs[:, :depth], buf[i, 0], preferred_element_type=f32)
-        value = value + jnp.dot(lhs[:, depth:], buf[i, 1], preferred_element_type=f32)
-        rows = value.shape[0] // parts
-        for p in range(parts):
-            target = outs[i * parts + p]
-            target[...] = value[p * rows : (p + 1) * rows].astype(target.dtype)
-
-
-def out_terms(heads, w_own, w_far, plan, first, amount, width, kind, parts=1):
-    opening = isinstance(heads, tuple)
+        outs[i][...] = value + jnp.dot(lhs[:, depth:], buf[i, 1], preferred_element_type=f32)
+
+
+def out_terms(heads, w_own, w_far, plan, first, amount, width):
     depth = w_own.shape[0]
-    rows = 2 * heads[0].size // (2 * depth) if opening else heads.shape[0]
+    rows = heads.shape[0]
     vmem = pl.BlockSpec(memory_space=pltpu.VMEM)
     anywhere = pl.BlockSpec(memory_space=pl.ANY)
-    args = list(heads) if opening else [heads]
-    shapes = [jax.ShapeDtypeStruct((rows // parts, width), kind)] * (amount * parts)
-    scratch = [
-        pltpu.VMEM((amount, 2, depth, width), bf16),
-        pltpu.SemaphoreType.DMA((2 * amount,)),
-    ]
-    if opening:
-        shapes.append(jax.ShapeDtypeStruct((rows, 2 * depth), bf16))
-        scratch += [pltpu.VMEM(heads[0].shape, f32), pltpu.VMEM((rows, 2 * depth), f32)]
     return pl.pallas_call(
-        functools.partial(out_kernel, first, amount, parts, opening),
-        in_specs=[pl.BlockSpec(memory_space=pltpu.SMEM)] + [vmem] * len(args) + [anywhere] * 2,
-        out_specs=[vmem] * len(shapes),
-        out_shape=shapes,
-        scratch_shapes=scratch,
+        functools.partial(out_kernel, first, amount),
+        in_specs=[pl.BlockSpec(memory_space=pltpu.SMEM), vmem] + [anywhere] * 2,
+        out_specs=[vmem] * amount,
+        out_shape=[jax.ShapeDtypeStruct((rows, width), f32)] * amount,
+        scratch_shapes=[
+            pltpu.VMEM((amount, 2, depth, width), bf16),
+            pltpu.SemaphoreType.DMA((amount, 2)),
+        ],
         cost_estimate=BESIDE,
         compiler_params=pltpu.CompilerParams(vmem_limit_bytes=VMEM_LIMIT),
-    )(plan, *args, w_own, w_far)
+    )(plan, heads, w_own, w_far)
 
 
 def attend_kernel(
@@ -296,7 +362,8 @@
                     suffix_far.at[row_ref[r]], page_buf.at[r], page_sem.at[r]
                 ).start()
 
-    fetch(0)
+    for j in range(prompts):
+        fetch(j)
     q_buf[...] = q_ref[...].astype(f32)
     position = lax.broadcasted_iota(jnp.int32, (beam_rows, page), 1)
     nt = (((1,), (1,)), ((), ()))
@@ -307,8 +374,6 @@
         for b in range(HALF):
             r = j * HALF + b
             pltpu.make_async_copy(suffix_own.at[0], page_buf.at[r], page_sem.at[r]).wait()
-        if j + 1 < prompts:
-            fetch(j + 1)
 
         def spread(ref, columns):
             return jnp.concatenate(
@@ -323,13 +388,15 @@
         cosine = spread(cos_ref, everything)
         sines = spread(sin_ref, everything)
         masks = [position < length_ref[j * HALF + b] for b in range(HALF)]
-        for k in range(KV):
-            spots = [
+        def place(k):
+            return [
                 (k * per_kv + t, slice((j * HALF + b) * heads_here, (j * HALF + b + 1) * heads_here))
                 for b in range(HALF)
                 for t in range(per_kv)
             ]
-            query = jnp.concatenate([q_buf[chip, rows, :] for chip, rows in spots], axis=0)
+
+        def score(k):
+            query = jnp.concatenate([q_buf[chip, rows, :] for chip, rows in place(k)], axis=0)
             turned = query * cosine + pltpu.roll(query, HD // 2, 1) * sines
             turned = (turned * HD ** (-0.5)).astype(bf16)
             prefix_scores = [
@@ -353,29 +420,31 @@
                 axis=0,
             )
             new_key = spread(new_ref, slice(k * HD, (k + 1) * HD))
-            new_value = spread(new_ref, slice((KV + k) * HD, (KV + k + 1) * HD))
             new_score = jnp.sum(turned.astype(f32) * new_key, axis=1, keepdims=True)
-            scores = prefix_scores + [page_scores]
+            return prefix_scores + [page_scores], new_score
+
+        def weigh(scores, new_score):
             highest = new_score
-            for score in scores:
-                highest = jnp.maximum(highest, jnp.max(score, axis=1, keepdims=True))
-            weights = [jnp.exp(score - highest) for score in scores]
+            for each in scores:
+                highest = jnp.maximum(highest, jnp.max(each, axis=1, keepdims=True))
+            weights = [jnp.exp(each - highest) for each in scores]
             new_weight = jnp.exp(new_score - highest)
             weight_sum = new_weight
             for weight in weights:
                 weight_sum = weight_sum + jnp.sum(weight, axis=1, keepdims=True)
+            return [weight.astype(bf16) for weight in weights], new_weight, weight_sum
+
+        def gather(k, weights, new_weight, weight_sum):
+            new_value = spread(new_ref, slice((KV + k) * HD, (KV + k + 1) * HD))
             weighted = new_weight.astype(bf16).astype(f32) * new_value
             for side in range(2):
                 weighted = weighted + jnp.dot(
-                    weights[side].astype(bf16),
-                    prefix_buf[j, side, 1, k],
-                    preferred_element_type=f32,
+                    weights[side], prefix_buf[j, side, 1, k], preferred_element_type=f32
                 )
-            page_weight = weights[2].astype(bf16)
             weighted = weighted + jnp.concatenate(
                 [
                     jnp.dot(
-                        page_weight[b * beam_rows : (b + 1) * beam_rows],
+                        weights[2][b * beam_rows : (b + 1) * beam_rows],
                         page_buf[j * HALF + b, 1, k],
                         preferred_element_type=f32,
                     )
@@ -384,8 +453,15 @@
                 axis=0,
             )
             result = weighted / weight_sum
-            for n, (chip, rows) in enumerate(spots):
+            for n, (chip, rows) in enumerate(place(k)):
                 o_buf[chip, rows, :] = result[n * heads_here : (n + 1) * heads_here]
+
+        ahead = score(0)
+        for k in range(KV):
+            now = ahead
+            if k + 1 < KV:
+                ahead = score(k + 1)
+            gather(k, *weigh(*now))
     out_ref[...] = o_buf[...].astype(bf16)
 
 
@@ -489,8 +565,8 @@
                 own_total = query_terms(own_total, fresh, w_query, None, plan, own_done)
                 far_total = list(query_terms(None, blocks, None, wq_far, plan, 0))
             else:
-                own_total, far_total = query_terms(
-                    own_total + far_total, fresh, w_query, wq_far, plan, own_done
+                own_total, far_total, *fetched = query_terms(
+                    own_total + far_total, fresh, w_query, wq_far, plan, own_done, None, s == hops
                 )
                 own_total, far_total = [own_total], [far_total]
             far_total = far_total or []
@@ -500,7 +576,6 @@
                 far_total, beside = beside[:1], beside[1:]
             if s == 2:
                 wo_send, suffix_in = tied(*beside, suffix_kv)
-                wo_far = send(wo_send, to_core)
                 suffix_far = send(suffix_in, to_core)
             own_done = len(blocks)
         if s < hops:
@@ -508,7 +583,7 @@
         else:
             blocks.append([(a, 0), (b, cut)])
     keep, give = query_terms(
-        own_total + far_total, blocks[own_done:], w_query, wq_far, plan, own_done, True
+        own_total + far_total, blocks[own_done:], w_query, wq_far, plan, own_done, *fetched
     )
     query = (keep + send(give, to_core)).astype(bf16).reshape(chips, -1, HD)
     same_core = [[2 * chip + side for chip in range(chips)] for side in range(2)]
@@ -518,22 +593,24 @@
             values, "tensor", split_axis=0, concat_axis=0, axis_index_groups=same_core, tiled=True
         )
 
-    query, suffix_far, wo_far = tied(query, suffix_far, wo_far)
+    query, suffix_far, wo_send = tied(query, suffix_far, wo_send)
+    wo_far = send(wo_send, to_core)
     heads = exchange(
         attend(exchange(query), cosine, sines, new_rows, prefix_kv, prefix_far, suffix_kv,
                suffix_far, source, page_row, page_len)
     ).reshape(-1, HD)
-    heads = (heads, send(heads, to_core))
-
     width = w_out.shape[1] // count
-
-    def out(heads, first, amount, kind, parts=1):
-        return out_terms(heads, w_out, wo_far, plan, chips + first, amount, width, kind, parts)
-
-    up, down, heads = tied(*out(heads, 0, 1, bf16, 2))
+    heads, w_whole = tied(heads, w_out)
+    columns = first_columns(w_whole, wo_far, plan, chips, width)
+    other, columns = tied(send(heads, to_core), columns)
+
+    def out(first, amount):
+        return out_terms(heads, w_out, wo_far, plan, chips + first, amount, width)
+
+    up, down, heads = tied(*opening_terms(heads, other, columns, plan, 2))
     a, b = send(up, onward), send(down, backward)
     for s in range(hops - 1, 0, -1):
-        up, down = out(heads, 1 + 2 * (hops - 1 - s), 2, f32)
+        up, down = out(1 + 2 * (hops - 1 - s), 2)
         a, b, up, down = tied(a, b, up, down)
         a, b = a.astype(f32), b.astype(f32)
         if s == hops - 1:
@@ -543,7 +620,7 @@
             up, down = up + a, down + b
         a, b = tied(up.astype(bf16), down.astype(bf16))
         a, b = send(a, onward), send(b, backward)
-    [own_term] = out(heads, chips - 1, 1, f32)
+    [own_term] = out(chips - 1, 1)
     a, b, own_term = tied(a, b, own_term)
     return (own_term + a.astype(f32) + b.astype(f32)).astype(bf16)
 

time: 126 us -> 123 us (0.976)
  local copies, waits for them, and re-layouts: 1.38 us -> 4.61 us
  waiting for transfers between devices: 26.7 us -> 23.5 us
  Pallas kernels: 53.4 us -> 51.1 us
    ppermute x23, waiting for transfers between devices: 26.7 us -> 23.5 us  [send(): return lax.ppermute(block, 'tensor', route)]
    unnamed x14 -> x12, local copies, waits for them, and re-layouts: 0.03 us -> 3.27 us
    pallas_call x5, Pallas kernels: 15.4 us -> 13.7 us  [query_terms(): pl.pallas_call(functools.partial(query_kernel, bases, first, far, bool(to...]
    pallas_call x1, Pallas kernels: 8.55 us -> 7.22 us  [attend(): pl.pallas_call(attend_kernel, in_specs=[smem] * 3 + [vmem] * 4 + [anywher...]
    pallas_call x5 -> x6, Pallas kernels: 15.5 us -> 16.1 us  [the longest x4 12.8 us: out_terms(): pl.pallas_call(functools.partial(out_kernel, first, amount), in_specs=[pl...]
  transfers between devices with their start and end apart: 23 -> 23, of which waited for: 17 -> 16; matrix products, arithmetic and copies ran while one was open for 1% -> 2% of each run, Pallas kernels for 34% -> 41%
where the time goes in v3:
time: 123 us; the launch traced here: 122 us
  Pallas kernels  51.1 us (42%)
  waiting for transfers between devices  23.5 us (19%)
  blocking collectives  22.9 us (19%)
  starting transfers between devices  18 us (15%)
  local copies, waits for them, and re-layouts  4.61 us (4%)
  other arithmetic  1.95 us (2%)
    ppermute x23, waiting for transfers between devices, send(): return lax.ppermute(block, 'tensor', route)  23.5 us
    all_to_all x2, blocking collectives, exchange(): lax.all_to_all(values, 'tensor', split_axis=0, concat_axis=0, axis_index_...  22.9 us
    ppermute x23, starting transfers between devices, send(): return lax.ppermute(block, 'tensor', route)  18 us
    pallas_call x2, Pallas kernels, others_half(): pl.pallas_call(functools.partial(split_kernel, chips, by_rows), in_specs=...  14 us
    pallas_call x5, Pallas kernels, query_terms(): pl.pallas_call(functools.partial(query_kernel, bases, first, far, bool(to...  13.7 us
    pallas_call x4, Pallas kernels, out_terms(): pl.pallas_call(functools.partial(out_kernel, first, amount), in_specs=[pl...  12.8 us
    pallas_call x1, Pallas kernels, attend(): pl.pallas_call(attend_kernel, in_specs=[smem] * 3 + [vmem] * 4 + [anywher...  7.22 us
    unnamed x12, local copies, waits for them, and re-layouts  3.27 us
  transfers between devices with their start and end apart: 23, of which 16 were waited for; matrix products, arithmetic and copies ran while one was open for 2% of the time, Pallas kernels for 41%

profile of v3, /device:TPU:0, one launch (start us, length us, event | category | flops | bytes accessed | tf_op | source)
XLA Modules:
  0.0 122.4 jit_solution(15492591064656371508)
XLA Ops:
  0.5 2.6 %collective-permute-start = (bf16[192,1024]{1,0:T(8,128)(2,1)}, bf16[192,1024]{1,0:T(8,128)(2,1)S(1)}, u32[]{:S(2)}, u32[]{:S(2)}) collective-permute-start(bf16[192,1024]{1,0:T(8,128)(2,1)} %refs_0_.3), channel_id=1, source_target_pairs={{0,4},{1,5},{4,8},{5,9},{8,12},{9,13},{12,14},{13,15},{14,10},{15,... | collective-permute-start | bytes 1179656 | tf_op jit(solution)/shard_map/ppermute | solution.py:32
  4.0 7.0 %shard_map.91 = bf16[8192,512]{1,0:T(8,128)(2,1)} custom-call(s32[17]{0:T(128)S(1)} %dynamic-slice_bitcast_fusion.plan_ref, bf16[16384,512]{1,0:T(8,128)(2,1)} %refs_2_.3), custom_call_target="tpu_custom_call" | custom-call | flops 1000 | bytes 1000 | tf_op jit(solution)/shard_map/pallas_call | solution.py:84
  14.5 1.6 %collective-permute-start.4 = (bf16[192,1024]{1,0:T(8,128)(2,1)S(1)}, bf16[192,1024]{1,0:T(8,128)(2,1)S(1)}, u32[]{:S(2)}, u32[]{:S(2)}) collective-permute-start(bf16[192,1024]{1,0:T(8,128)(2,1)S(1)} %collective-permute-done.refs_1_), channel_id=1, source_target_pairs={{0,4},{1,5},{4,8},{5,9},{8,12},{9,13},{12,14},{13,15},{14,10},{15,... | collective-permute-start | bytes 1179656 | tf_op jit(solution)/shard_map/ppermute | solution.py:32
  16.5 2.8 %shard_map.92.refs_3_ = f32[192,512]{1,0:T(8,128)S(1)} custom-call(s32[17]{0:T(128)S(1)} %dynamic-slice_bitcast_fusion.plan_ref, bf16[192,1024]{1,0:T(8,128)(2,1)S(1)} %copy-done.1, bf16[192,1024]{1,0:T(8,128)(2,1)S(1)} %collective-permute-done.refs_1_, bf16[192,1024]{1,0:T(8,128)(2,1)S(1)} %collective-permute-done.1.refs_2_, bf16[16384,512]{1,0:T(8,128)(2,1)} %refs_2_.3), custom_call_target="tpu_custom_call" | custom-call | flops 1000 | bytes 1000 | tf_op jit(solution)/shard_map/pallas_call | solution.py:201
  19.3 7.0 %shard_map.93 = bf16[512,8192]{1,0:T(8,128)(2,1)} custom-call(s32[17]{0:T(128)S(1)} %dynamic-slice_bitcast_fusion.plan_ref, bf16[512,16384]{1,0:T(8,128)(2,1)} %w_own.8), custom_call_target="tpu_custom_call" | custom-call | flops 1000 | bytes 1000 | tf_op jit(solution)/shard_map/pallas_call | solution.py:84
  29.3 2.5 %shard_map.94.refs_4_ = f32[192,512]{1,0:T(8,128)S(1)} custom-call(s32[17]{0:T(128)S(1)} %dynamic-slice_bitcast_fusion.plan_ref, bf16[192,1024]{1,0:T(8,128)(2,1)S(1)} %collective-permute-done.4.refs_0_.refs_3_, bf16[192,1024]{1,0:T(8,128)(2,1)S(1)} %collective-permute-done.5.refs_1_.refs_4_, bf16[16384,512]{1,0:T(8,128)(2,1)} %refs_2_.3, ...), custom_call_target="tpu_custom_call" | custom-call | flops 1000 | bytes 1000 | tf_op jit(solution)/shard_map/pallas_call | solution.py:201
  31.9 3.2 %copy-done.2 = bf16[8192,512]{1,0:T(8,128)(2,1)} copy-done((bf16[8192,512]{1,0:T(8,128)(2,1)}, bf16[8192,512]{1,0:T(8,128)(2,1)S(1)}, u32[]{:S(2)}) %copy-start.2) | copy-done | bytes 8388632
  35.1 3.5 %shard_map.95.refs_5_ = f32[192,512]{1,0:T(8,128)S(1)} custom-call(s32[17]{0:T(128)S(1)} %dynamic-slice_bitcast_fusion.plan_ref, bf16[192,1024]{1,0:T(8,128)(2,1)S(1)} %copy-done.1, bf16[192,1024]{1,0:T(8,128)(2,1)S(1)} %collective-permute-done.refs_1_, bf16[192,1024]{1,0:T(8,128)(2,1)S(1)} %collective-permute-done.1.refs_2_, ...), custom_call_target="tpu_custom_call" | custom-call | flops 1000 | bytes 1000 | tf_op jit(solution)/shard_map/pallas_call | solution.py:201
  40.7 1.6 %collective-permute-start.9 = (bf16[96,1024]{1,0:T(8,128)(2,1)S(1)}, bf16[96,1024]{1,0:T(8,128)(2,1)S(1)}, u32[]{:S(2)}, u32[]{:S(2)}) collective-permute-start(bf16[96,1024]{1,0:T(8,128)(2,1)S(1)} %slice.20), channel_id=1, source_target_pairs={{0,4},{1,5},{4,8},{5,9},{8,12},{9,13},{12,14},{13,15},{14,10},{15,... | collective-permute-start | bytes 589832 | tf_op jit(solution)/shard_map/ppermute | solution.py:32
  42.3 3.5 %shard_map.96 = (f32[192,512]{1,0:T(8,128)S(1)}, f32[192,512]{1,0:T(8,128)S(1)}, bf16[2,1024,512]{2,1,0:T(8,128)(2,1)S(1)}) custom-call(s32[17]{0:T(128)S(1)} %dynamic-slice_bitcast_fusion.plan_ref, bf16[192,1024]{1,0:T(8,128)(2,1)S(1)} %collective-permute-done.6.refs_0_, bf16[192,1024]{1,0:T(8,128)(2,1)S(1)} %collective-permute-done.7.refs_1_, ...), custom_call_target="tpu_custom_call" | custom-call | flops 1000 | bytes 1000 | tf_op jit(solution)/shard_map/pallas_call | solution.py:201
  48.3 1.7 %collective-permute-done.11 = f32[768,128]{1,0:T(8,128)S(1)} collective-permute-done((f32[768,128]{1,0:T(8,128)S(1)}, f32[768,128]{1,0:T(8,128)S(1)}, u32[]{:S(2)}, u32[]{:S(2)}) %collective-permute-start.11) | collective-permute-done | bytes 393248 | tf_op jit(solution)/shard_map/ppermute | solution.py:32
  50.3 12.2 %all_to_all.10.q_ref = bf16[8,96,128]{2,1,0:T(8,128)(2,1)S(1)} all-to-all(bf16[8,96,128]{2,1,0:T(8,128)(2,1)S(1)} %bitcast.6), channel_id=1, replica_groups={{0,2,4,6,8,10,12,14},{1,3,5,7,9,11,13,15},{16,18,20,22,24,26,28,30},{17..., dimensions={0} | all-to-all | bytes 393216 | tf_op jit(solution)/shard_map/all_to_all | solution.py:592
  62.5 7.2 %shard_map.98 = bf16[8,96,128]{2,1,0:T(8,128)(2,1)S(1)} custom-call(s32[12]{0:T(128)S(1)} %get-tuple-element.73.source_ref, s32[12]{0:T(128)S(1)} %fusion.2.row_ref, s32[12]{0:T(128)S(1)} %get-tuple-element.75.length_ref, bf16[8,96,128]{2,1,0:T(8,128)(2,1)S(1)} %all_to_all.10.q_ref, f32[12,128]{1,0:T(8,128)S(1)} %get-tuple-element.101.cos_ref, ...), custom_call_target="tpu_custom_call" | custom-call | flops 503316480 | bytes 12582912 | tf_op jit(solution)/shard_map/pallas_call | solution.py:478
  69.7 10.6 %all_to_all.11 = bf16[8,96,128]{2,1,0:T(8,128)(2,1)S(1)} all-to-all(bf16[8,96,128]{2,1,0:T(8,128)(2,1)S(1)} %shard_map.98), channel_id=1, replica_groups={{0,2,4,6,8,10,12,14},{1,3,5,7,9,11,13,15},{16,18,20,22,24,26,28,30},{17..., dimensions={0} | all-to-all | bytes 393216 | tf_op jit(solution)/shard_map/all_to_all | solution.py:592
  80.4 2.1 %shard_map.99.columns_ref = bf16[2,512,1024]{2,1,0:T(8,128)(2,1)S(1)} custom-call(s32[17]{0:T(128)S(1)} %dynamic-slice_bitcast_fusion.plan_ref, bf16[512,16384]{1,0:T(8,128)(2,1)} %w_own.8, bf16[512,8192]{1,0:T(8,128)(2,1)} %collective-permute-done.14.w_far), custom_call_target="tpu_custom_call" | custom-call | flops 1000 | bytes 1000 | tf_op jit(solution)/shard_map/pallas_call | solution.py:240
  83.8 2.0 %collective-permute-start.16 = (bf16[96,1024]{1,0:T(8,128)(2,1)S(1)}, bf16[96,1024]{1,0:T(8,128)(2,1)S(1)}, u32[]{:S(2)}, u32[]{:S(2)}) collective-permute-start(bf16[96,1024]{1,0:T(8,128)(2,1)S(1)} %get-tuple-element.112), channel_id=1, source_target_pairs={{0,2},{1,3},{4,0},{5,1},{8,4},{9,5},{12,8},{13,9},{14,12},{15,13},... | collective-permute-start | bytes 589832 | tf_op jit(solution)/shard_map/ppermute | solution.py:32
  85.8 3.4 %shard_map.101 = (f32[192,1024]{1,0:T(8,128)S(1)}, f32[192,1024]{1,0:T(8,128)S(1)}) custom-call(s32[17]{0:T(128)S(1)} %dynamic-slice_bitcast_fusion.plan_ref, bf16[192,1024]{1,0:T(8,128)(2,1)S(1)} %get-tuple-element.113.lhs, bf16[512,16384]{1,0:T(8,128)(2,1)} %w_own.8, bf16[512,8192]{1,0:T(8,128)(2,1)} %collective-permute-done.14.w_far), custom_call_target="tpu_custom_call" | custom-call | flops 1000 | bytes 1000 | tf_op jit(solution)/shard_map/pallas_call | solution.py:315
  89.2 1.9 %collective-permute-done.15 = bf16[96,1024]{1,0:T(8,128)(2,1)S(1)} collective-permute-done((bf16[96,1024]{1,0:T(8,128)(2,1)S(1)}, bf16[96,1024]{1,0:T(8,128)(2,1)S(1)}, u32[]{:S(2)}, u32[]{:S(2)}) %collective-permute-start.15) | collective-permute-done | bytes 196640 | tf_op jit(solution)/shard_map/ppermute | solution.py:32
  93.5 3.4 %shard_map.102 = (f32[192,1024]{1,0:T(8,128)S(1)}, f32[192,1024]{1,0:T(8,128)S(1)}) custom-call(s32[17]{0:T(128)S(1)} %dynamic-slice_bitcast_fusion.plan_ref, bf16[192,1024]{1,0:T(8,128)(2,1)S(1)} %get-tuple-element.113.lhs, bf16[512,16384]{1,0:T(8,128)(2,1)} %w_own.8, bf16[512,8192]{1,0:T(8,128)(2,1)} %collective-permute-done.14.w_far), custom_call_target="tpu_custom_call" | custom-call | flops 1000 | bytes 1000 | tf_op jit(solution)/shard_map/pallas_call | solution.py:315
  96.8 5.4 %collective-permute-done.17 = bf16[192,1024]{1,0:T(8,128)(2,1)S(1)} collective-permute-done((bf16[192,1024]{1,0:T(8,128)(2,1)S(1)}, bf16[192,1024]{1,0:T(8,128)(2,1)S(1)}, u32[]{:S(2)}, u32[]{:S(2)}) %collective-permute-start.17) | collective-permute-done | bytes 393248 | tf_op jit(solution)/shard_map/ppermute | solution.py:32
  104.6 3.4 %shard_map.103 = (f32[192,1024]{1,0:T(8,128)S(1)}, f32[192,1024]{1,0:T(8,128)S(1)}) custom-call(s32[17]{0:T(128)S(1)} %dynamic-slice_bitcast_fusion.plan_ref, bf16[192,1024]{1,0:T(8,128)(2,1)S(1)} %get-tuple-element.113.lhs, bf16[512,16384]{1,0:T(8,128)(2,1)} %w_own.8, bf16[512,8192]{1,0:T(8,128)(2,1)} %collective-permute-done.14.w_far), custom_call_target="tpu_custom_call" | custom-call | flops 1000 | bytes 1000 | tf_op jit(solution)/shard_map/pallas_call | solution.py:315
  108.0 4.3 %collective-permute-done.19 = bf16[192,1024]{1,0:T(8,128)(2,1)S(1)} collective-permute-done((bf16[192,1024]{1,0:T(8,128)(2,1)S(1)}, bf16[192,1024]{1,0:T(8,128)(2,1)S(1)}, u32[]{:S(2)}, u32[]{:S(2)}) %collective-permute-start.19) | collective-permute-done | bytes 393248 | tf_op jit(solution)/shard_map/ppermute | solution.py:32
  114.6 2.7 %shard_map.104 = f32[192,1024]{1,0:T(8,128)S(1)} custom-call(s32[17]{0:T(128)S(1)} %dynamic-slice_bitcast_fusion.plan_ref, bf16[192,1024]{1,0:T(8,128)(2,1)S(1)} %get-tuple-element.113.lhs, bf16[512,16384]{1,0:T(8,128)(2,1)} %w_own.8, bf16[512,8192]{1,0:T(8,128)(2,1)} %collective-permute-done.14.w_far), custom_call_target="tpu_custom_call" | custom-call | flops 1000 | bytes 1000 | tf_op jit(solution)/shard_map/pallas_call | solution.py:315
  117.3 4.0 %collective-permute-done.21 = bf16[192,1024]{1,0:T(8,128)(2,1)S(1)} collective-permute-done((bf16[192,1024]{1,0:T(8,128)(2,1)S(1)}, bf16[192,1024]{1,0:T(8,128)(2,1)S(1)}, u32[]{:S(2)}, u32[]{:S(2)}) %collective-permute-start.21) | collective-permute-done | bytes 393248 | tf_op jit(solution)/shard_map/ppermute | solution.py:32
  (82 shorter events, 22.5 us)
Async XLA Ops:
  0.0 14.5 %collective-permute-start.2 = (bf16[1,3,2,4,512,128]{5,4,3,2,1,0:T(8,128)(2,1)}, bf16[1,3,2,4,512,128]{5,4,3,2,1,0:T(8,128)(2,1)}, u32[]{:S(2)}, u32[]{:S(2)}) collective-permute-start(bf16[1,3,2,4,512,128]{5,4,3,2,1,0:T(8,128)(2,1)} %prefix_own.1), channel_id=1, source_target_pairs={{0,1},{1,0},{2,3},{3,2},{4,5},{5,4},{6,7},{7,6},{8,9},{9,8},{10,11... | collective-permute-start | bytes 9437192 | tf_op jit(solution)/shard_map/ppermute | solution.py:32
  0.5 12.5 %collective-permute-start = (bf16[192,1024]{1,0:T(8,128)(2,1)}, bf16[192,1024]{1,0:T(8,128)(2,1)S(1)}, u32[]{:S(2)}, u32[]{:S(2)}) collective-permute-start(bf16[192,1024]{1,0:T(8,128)(2,1)} %refs_0_.3), channel_id=1, source_target_pairs={{0,4},{1,5},{4,8},{5,9},{8,12},{9,13},{12,14},{13,15},{14,10},{15,... | collective-permute-start | bytes 1179656 | tf_op jit(solution)/shard_map/ppermute | solution.py:32
  3.0 11.5 %collective-permute-start.1 = (bf16[192,1024]{1,0:T(8,128)(2,1)}, bf16[192,1024]{1,0:T(8,128)(2,1)S(1)}, u32[]{:S(2)}, u32[]{:S(2)}) collective-permute-start(bf16[192,1024]{1,0:T(8,128)(2,1)} %refs_0_.3), channel_id=1, source_target_pairs={{0,2},{1,3},{4,0},{5,1},{8,4},{9,5},{12,8},{13,9},{14,12},{15,13},... | collective-permute-start | bytes 1179656 | tf_op jit(solution)/shard_map/ppermute | solution.py:32
  3.0 8.4 %collective-permute-start.3 = (s32[12]{0:T(128)}, s32[12]{0:T(128)S(1)}, u32[]{:S(2)}, u32[]{:S(2)}) collective-permute-start(s32[12]{0:T(128)} %param.16), channel_id=1, source_target_pairs={{0,1},{1,0},{2,3},{3,2},{4,5},{5,4},{6,7},{7,6},{8,9},{9,8},{10,11... | collective-permute-start | bytes 152 | tf_op jit(solution)/shard_map/ppermute | solution.py:32
  14.5 17.3 %collective-permute-start.8 = (bf16[8192,512]{1,0:T(8,128)(2,1)}, bf16[8192,512]{1,0:T(8,128)(2,1)S(1)}, u32[]{:S(2)}, u32[]{:S(2)}) collective-permute-start(bf16[8192,512]{1,0:T(8,128)(2,1)} %shard_map.91), channel_id=1, source_target_pairs={{0,1},{1,0},{2,3},{3,2},{4,5},{5,4},{6,7},{7,6},{8,9},{9,8},{10,11... | collective-permute-start | bytes 25165832 | tf_op jit(solution)/shard_map/ppermute | solution.py:32
  14.5 11.9 %collective-permute-start.4 = (bf16[192,1024]{1,0:T(8,128)(2,1)S(1)}, bf16[192,1024]{1,0:T(8,128)(2,1)S(1)}, u32[]{:S(2)}, u32[]{:S(2)}) collective-permute-start(bf16[192,1024]{1,0:T(8,128)(2,1)S(1)} %collective-permute-done.refs_1_), channel_id=1, source_target_pairs={{0,4},{1,5},{4,8},{5,9},{8,12},{9,13},{12,14},{13,15},{14,10},{15,... | collective-permute-start | bytes 1179656 | tf_op jit(solution)/shard_map/ppermute | solution.py:32
  16.1 11.2 %collective-permute-start.5 = (bf16[192,1024]{1,0:T(8,128)(2,1)S(1)}, bf16[192,1024]{1,0:T(8,128)(2,1)S(1)}, u32[]{:S(2)}, u32[]{:S(2)}) collective-permute-start(bf16[192,1024]{1,0:T(8,128)(2,1)S(1)} %collective-permute-done.1.refs_2_), channel_id=1, source_target_pairs={{0,2},{1,3},{4,0},{5,1},{8,4},{9,5},{12,8},{13,9},{14,12},{15,13},... | collective-permute-start | bytes 1179656 | tf_op jit(solution)/shard_map/ppermute | solution.py:32
  27.3 22.7 %collective-permute-start.12 = (bf16[12,2,4,256,128]{4,3,2,1,0:T(8,128)(2,1)}, bf16[12,2,4,256,128]{4,3,2,1,0:T(8,128)(2,1)}, u32[]{:S(2)}, u32[]{:S(2)}) collective-permute-start(bf16[12,2,4,256,128]{4,3,2,1,0:T(8,128)(2,1)} %suffix_own.1), channel_id=1, source_target_pairs={{0,1},{1,0},{2,3},{3,2},{4,5},{5,4},{6,7},{7,6},{8,9},{9,8},{10,11... | collective-permute-start | bytes 18874376 | tf_op jit(solution)/shard_map/ppermute | solution.py:32
  27.3 11.5 %collective-permute-start.6 = (bf16[192,1024]{1,0:T(8,128)(2,1)S(1)}, bf16[192,1024]{1,0:T(8,128)(2,1)S(1)}, u32[]{:S(2)}, u32[]{:S(2)}) collective-permute-start(bf16[192,1024]{1,0:T(8,128)(2,1)S(1)} %collective-permute-done.4.refs_0_.refs_3_), channel_id=1, source_target_pairs={{0,4},{1,5},{4,8},{5,9},{8,12},{9,13},{12,14},{13,15},{14,10},{15,... | collective-permute-start | bytes 1179656 | tf_op jit(solution)/shard_map/ppermute | solution.py:32
  28.9 11.2 %collective-permute-start.7 = (bf16[192,1024]{1,0:T(8,128)(2,1)S(1)}, bf16[192,1024]{1,0:T(8,128)(2,1)S(1)}, u32[]{:S(2)}, u32[]{:S(2)}) collective-permute-start(bf16[192,1024]{1,0:T(8,128)(2,1)S(1)} %collective-permute-done.5.refs_1_.refs_4_), channel_id=1, source_target_pairs={{0,2},{1,3},{4,0},{5,1},{8,4},{9,5},{12,8},{13,9},{14,12},{15,13},... | collective-permute-start | bytes 1179656 | tf_op jit(solution)/shard_map/ppermute | solution.py:32
  40.2 6.3 %collective-permute-start.10 = (bf16[96,1024]{1,0:T(8,128)(2,1)S(1)}, bf16[96,1024]{1,0:T(8,128)(2,1)S(1)}, u32[]{:S(2)}, u32[]{:S(2)}) collective-permute-start(bf16[96,1024]{1,0:T(8,128)(2,1)S(1)} %slice.21), channel_id=1, source_target_pairs={{0,2},{1,3},{4,0},{5,1},{8,4},{9,5},{12,8},{13,9},{14,12},{15,13},... | collective-permute-start | bytes 589832 | tf_op jit(solution)/shard_map/ppermute | solution.py:32
  40.7 21.8 %copy-start = (bf16[1,3,2,4,512,128]{5,4,3,2,1,0:T(8,128)(2,1)S(1)}, bf16[1,3,2,4,512,128]{5,4,3,2,1,0:T(8,128)(2,1)}, u32[]{:S(2)}) copy-start(bf16[1,3,2,4,512,128]{5,4,3,2,1,0:T(8,128)(2,1)} %prefix_own.1) | copy-start | bytes 9437188
  40.7 6.0 %collective-permute-start.9 = (bf16[96,1024]{1,0:T(8,128)(2,1)S(1)}, bf16[96,1024]{1,0:T(8,128)(2,1)S(1)}, u32[]{:S(2)}, u32[]{:S(2)}) collective-permute-start(bf16[96,1024]{1,0:T(8,128)(2,1)S(1)} %slice.20), channel_id=1, source_target_pairs={{0,4},{1,5},{4,8},{5,9},{8,12},{9,13},{12,14},{13,15},{14,10},{15,... | collective-permute-start | bytes 589832 | tf_op jit(solution)/shard_map/ppermute | solution.py:32
  48.2 1.8 %collective-permute-start.11 = (f32[768,128]{1,0:T(8,128)S(1)}, f32[768,128]{1,0:T(8,128)S(1)}, u32[]{:S(2)}, u32[]{:S(2)}) collective-permute-start(f32[768,128]{1,0:T(8,128)S(1)} %get-tuple-element.96), channel_id=1, source_target_pairs={{0,1},{1,0},{2,3},{3,2},{4,5},{5,4},{6,7},{7,6},{8,9},{9,8},{10,11... | collective-permute-start | bytes 1179656 | tf_op jit(solution)/shard_map/ppermute | solution.py:32
  50.1 30.3 %collective-permute-start.14 = (bf16[512,8192]{1,0:T(8,128)(2,1)}, bf16[512,8192]{1,0:T(8,128)(2,1)}, u32[]{:S(2)}, u32[]{:S(2)}) collective-permute-start(bf16[512,8192]{1,0:T(8,128)(2,1)} %shard_map.93), channel_id=1, source_target_pairs={{0,1},{1,0},{2,3},{3,2},{4,5},{5,4},{6,7},{7,6},{8,9},{9,8},{10,11... | collective-permute-start | bytes 25165832 | tf_op jit(solution)/shard_map/ppermute | solution.py:32
  80.4 2.1 %collective-permute-start.13 = (bf16[768,128]{1,0:T(8,128)(2,1)S(1)}, bf16[768,128]{1,0:T(8,128)(2,1)S(1)}, u32[]{:S(2)}, u32[]{:S(2)}) collective-permute-start(bf16[768,128]{1,0:T(8,128)(2,1)S(1)} %bitcast.4), channel_id=1, source_target_pairs={{0,1},{1,0},{2,3},{3,2},{4,5},{5,4},{6,7},{7,6},{8,9},{9,8},{10,11... | collective-permute-start | bytes 589832 | tf_op jit(solution)/shard_map/ppermute | solution.py:32
  83.7 7.4 %collective-permute-start.15 = (bf16[96,1024]{1,0:T(8,128)(2,1)S(1)}, bf16[96,1024]{1,0:T(8,128)(2,1)S(1)}, u32[]{:S(2)}, u32[]{:S(2)}) collective-permute-start(bf16[96,1024]{1,0:T(8,128)(2,1)S(1)} %get-tuple-element.111), channel_id=1, source_target_pairs={{0,4},{1,5},{4,8},{5,9},{8,12},{9,13},{12,14},{13,15},{14,10},{15,... | collective-permute-start | bytes 589832 | tf_op jit(solution)/shard_map/ppermute | solution.py:32
  83.8 7.4 %collective-permute-start.16 = (bf16[96,1024]{1,0:T(8,128)(2,1)S(1)}, bf16[96,1024]{1,0:T(8,128)(2,1)S(1)}, u32[]{:S(2)}, u32[]{:S(2)}) collective-permute-start(bf16[96,1024]{1,0:T(8,128)(2,1)S(1)} %get-tuple-element.112), channel_id=1, source_target_pairs={{0,2},{1,3},{4,0},{5,1},{8,4},{9,5},{12,8},{13,9},{14,12},{15,13},... | collective-permute-start | bytes 589832 | tf_op jit(solution)/shard_map/ppermute | solution.py:32
  91.4 10.8 %collective-permute-start.17 = (bf16[192,1024]{1,0:T(8,128)(2,1)S(1)}, bf16[192,1024]{1,0:T(8,128)(2,1)S(1)}, u32[]{:S(2)}, u32[]{:S(2)}) collective-permute-start(bf16[192,1024]{1,0:T(8,128)(2,1)S(1)} %pad_maximum_fusion), channel_id=1, source_target_pairs={{0,4},{1,5},{4,8},{5,9},{8,12},{9,13},{12,14},{13,15},{14,10},{15,... | collective-permute-start | bytes 1179656 | tf_op jit(solution)/shard_map/ppermute | solution.py:32
  92.1 10.2 %collective-permute-start.18 = (bf16[192,1024]{1,0:T(8,128)(2,1)S(1)}, bf16[192,1024]{1,0:T(8,128)(2,1)S(1)}, u32[]{:S(2)}, u32[]{:S(2)}) collective-permute-start(bf16[192,1024]{1,0:T(8,128)(2,1)S(1)} %pad_maximum_fusion.1), channel_id=1, source_target_pairs={{0,2},{1,3},{4,0},{5,1},{8,4},{9,5},{12,8},{13,9},{14,12},{15,13},... | collective-permute-start | bytes 1179656 | tf_op jit(solution)/shard_map/ppermute | solution.py:32
  102.5 9.8 %collective-permute-start.19 = (bf16[192,1024]{1,0:T(8,128)(2,1)S(1)}, bf16[192,1024]{1,0:T(8,128)(2,1)S(1)}, u32[]{:S(2)}, u32[]{:S(2)}) collective-permute-start(bf16[192,1024]{1,0:T(8,128)(2,1)S(1)} %add_convert_fusion.4), channel_id=1, source_target_pairs={{0,4},{1,5},{4,8},{5,9},{8,12},{9,13},{12,14},{13,15},{14,10},{15,... | collective-permute-start | bytes 1179656 | tf_op jit(solution)/shard_map/ppermute | solution.py:32
  103.2 9.2 %collective-permute-start.20 = (bf16[192,1024]{1,0:T(8,128)(2,1)S(1)}, bf16[192,1024]{1,0:T(8,128)(2,1)S(1)}, u32[]{:S(2)}, u32[]{:S(2)}) collective-permute-start(bf16[192,1024]{1,0:T(8,128)(2,1)S(1)} %add_convert_fusion.3), channel_id=1, source_target_pairs={{0,2},{1,3},{4,0},{5,1},{8,4},{9,5},{12,8},{13,9},{14,12},{15,13},... | collective-permute-start | bytes 1179656 | tf_op jit(solution)/shard_map/ppermute | solution.py:32
  112.5 8.8 %collective-permute-start.21 = (bf16[192,1024]{1,0:T(8,128)(2,1)S(1)}, bf16[192,1024]{1,0:T(8,128)(2,1)S(1)}, u32[]{:S(2)}, u32[]{:S(2)}) collective-permute-start(bf16[192,1024]{1,0:T(8,128)(2,1)S(1)} %add_convert_fusion.2), channel_id=1, source_target_pairs={{0,4},{1,5},{4,8},{5,9},{8,12},{9,13},{12,14},{13,15},{14,10},{15,... | collective-permute-start | bytes 1179656 | tf_op jit(solution)/shard_map/ppermute | solution.py:32
  113.7 7.8 %collective-permute-start.22 = (bf16[192,1024]{1,0:T(8,128)(2,1)S(1)}, bf16[192,1024]{1,0:T(8,128)(2,1)S(1)}, u32[]{:S(2)}, u32[]{:S(2)}) collective-permute-start(bf16[192,1024]{1,0:T(8,128)(2,1)S(1)} %add_convert_fusion.1), channel_id=1, source_target_pairs={{0,2},{1,3},{4,0},{5,1},{8,4},{9,5},{12,8},{13,9},{14,12},{15,13},... | collective-permute-start | bytes 1179656 | tf_op jit(solution)/shard_map/ppermute | solution.py:32
  (5 other events, 37.2 us)
